TPU v7x, 32 devices: a whole 2x2x4 slice. The times are simulated.
32 devices in a mesh: replica: 4 (over x, core), fsdp: 8 (over z, y).
Axes of the slice: x: 2, y: 2, z: 4, core: 2. Of those that a mesh axis runs over, the one named last changes fastest.
Arguments:
- frag_index: int32 [8], replicated, may hold values from 0 to 7, as said below
- inner_step: int32 [8], replicated, may hold values from 1 to 8, as said below
- inner_params: float32 [4, 8, 65536], P('replica', None, 'fsdp'), may hold values from -6 to 6
- grads: bfloat16 [4, 8, 65536], P('replica', None, 'fsdp'), may hold values from -6 to 6
- adam_first: float32 [4, 8, 65536], P('replica', None, 'fsdp'), may hold values from -4 to 4
- adam_second: float32 [4, 8, 65536], P('replica', None, 'fsdp'), may hold values from 0.01 to 1
- outer_params: float32 [8, 65536], P(None, 'fsdp'), may hold values from -6 to 6
- outer_momentum: float32 [8, 65536], P(None, 'fsdp'), may hold values from -6 to 6
Outputs:
- new_inner: float32 [4, 8, 65536], P('replica', None, 'fsdp')
- new_first: float32 [4, 8, 65536], P('replica', None, 'fsdp')
- new_second: float32 [4, 8, 65536], P('replica', None, 'fsdp')
- new_outer: float32 [8, 65536], P(None, 'fsdp')
- new_momentum: float32 [8, 65536], P(None, 'fsdp')
- refreshed: bfloat16 [65536], replicated
Inputs may be any that keep to these rules, and one draw needn't show every extreme that they name: `frag_index`: each fragment number exactly once. `inner_step`: each count of 1 to 8 exactly once.
All inputs are finite; a program needn't handle non-finite values.
Results may differ from a plain program's by a relative error of at most 0.00075.
Values may be sent and summed in bfloat16 or wider, within the bound.
No kernel may reach another device: no remote copies, remote signals or barrier semaphores. Data moves between devices by JAX's collectives and lax.ppermute only.
A program may use at most 64 MiB of HBM per device.

v0:
```python
import jax
import jax.numpy as jnp
from jax import lax
from jax.sharding import PartitionSpec as P

beta_first = 0.9
beta_second = 0.95
adam_eps = 1e-08
inner_rate = 0.05
decay_rate = 0.1
outer_rate = 0.7
momentum_keep = 0.9
mix_local = 0.5


def nesterov(outer_row, moment_row, mean_drift):
    new_moment_row = momentum_keep * moment_row + mean_drift
    new_outer_row = outer_row - outer_rate * (mean_drift + momentum_keep * new_moment_row)
    return (new_outer_row, new_moment_row)


def on_device(
    frag_index,
    inner_step,
    inner_params,
    grads,
    adam_first,
    adam_second,
    outer_params,
    outer_momentum,
):
    fragment = frag_index[0]
    replicas = lax.axis_size("replica")
    inner_row = lax.dynamic_index_in_dim(inner_params[0], fragment, 0, keepdims=False)
    outer_row = lax.dynamic_index_in_dim(outer_params, fragment, 0, keepdims=False)
    moment_row = lax.dynamic_index_in_dim(outer_momentum, fragment, 0, keepdims=False)
    drift = outer_row - inner_row
    summed = lax.psum(drift, "replica")
    new_outer_row, new_moment_row = nesterov(outer_row, moment_row, summed / replicas)
    refreshed_shard = new_outer_row.astype(jnp.bfloat16)
    refreshed = lax.all_gather(refreshed_shard, "fsdp", axis=0, tiled=True)
    step_count = inner_step.astype(jnp.float32)[None, :, None]
    grad_wide = grads.astype(jnp.float32)
    first_moment = beta_first * adam_first + (1.0 - beta_first) * grad_wide
    second_moment = beta_second * adam_second + (1.0 - beta_second) * grad_wide * grad_wide
    first_fix = 1.0 - jnp.power(jnp.float32(beta_first), step_count)
    second_fix = 1.0 - jnp.power(jnp.float32(beta_second), step_count)
    stepped = inner_params * (1.0 - inner_rate * decay_rate) - inner_rate * (
        first_moment / first_fix
    ) / (jnp.sqrt(second_moment / second_fix) + adam_eps)
    stepped_row = lax.dynamic_index_in_dim(stepped, fragment, 1, keepdims=False)
    blended = (
        mix_local * stepped_row + (1.0 - mix_local) * refreshed_shard.astype(jnp.float32)[None, :]
    )
    new_inner = lax.dynamic_update_index_in_dim(stepped, blended, fragment, 1)
    new_outer = lax.dynamic_update_index_in_dim(outer_params, new_outer_row, fragment, 0)
    new_momentum = lax.dynamic_update_index_in_dim(outer_momentum, new_moment_row, fragment, 0)
    return (new_inner, first_moment, second_moment, new_outer, new_momentum, refreshed)


def solution(mesh):
    return jax.shard_map(
        on_device,
        mesh=mesh,
        in_specs=(
            P(),
            P(),
            P("replica", None, "fsdp"),
            P("replica", None, "fsdp"),
            P("replica", None, "fsdp"),
            P("replica", None, "fsdp"),
            P(None, "fsdp"),
            P(None, "fsdp"),
        ),
        out_specs=(
            P("replica", None, "fsdp"),
            P("replica", None, "fsdp"),
            P("replica", None, "fsdp"),
            P(None, "fsdp"),
            P(None, "fsdp"),
            P(),
        ),
        check_vma=False,
    )
```

profile of v0, /device:TPU:0, one launch (start us, length us, event | category | flops | bytes accessed | tf_op | source)
XLA Modules:
  0.0 48.8 jit_solution(1343754674434954777)
XLA Ops:
  0.6 0.0 copy-start.4
  0.6 0.0 copy-start.7
  0.7 1.0 %copy.21 = f32[8,8192]{1,0:T(8,128)S(1)} copy(f32[8,8192]{1,0:T(8,128)} %param.15) | data formatting | bytes 524288
  1.7 0.0 copy-done.4
  1.7 0.0 copy-start.8
  1.7 0.0 copy-start.9
  1.7 0.0 copy-start.2
  1.7 0.0 copy-start.6
  1.7 0.0 copy-start.5
  1.7 0.6 %copy-done.8 = s32[8]{0:T(128)S(1)} copy-done((s32[8]{0:T(128)S(1)}, s32[8]{0:T(128)}, u32[]{:S(2)}) %copy-start.8) | copy-done | bytes 56
  2.4 0.0 copy-done.9
  2.5 0.2 copy-done.2
  2.7 12.9 %psum.7 = f32[8192]{0:T(1024)S(1)} all-reduce(f32[8192]{0:T(1024)S(1)} %sub.20), channel_id=1, replica_groups=mesh['replica'=4,'fsdp'=8] {'replica'}, use_global_device_ids=true, to_apply=%region_0.1 | all-reduce | flops 8192 | bytes 65536 | tf_op jit(solution)/shard_map/psum | solution.py:38
  15.7 0.0 copy-done.7
  15.7 0.0 copy-done.6
  15.7 0.0 copy-done.5
  15.7 1.0 %divide_subtract_fusion = (f32[1,8,8192]{2,1,0:T(8,128)S(1)}, f32[1,8,8192]{2,1,0:T(8,128)}, f32[1,8,8192]{2,1,0:T(8,128)}) fusion(f32[1,8,8192]{2,1,0:T(8,128)S(1)} %copy-done.2, f32[8]{0:T(128)S(1)} %get-tuple-element.14, f32[8]{0:T(128)S(1)} %get-tuple-element.13, bf16[1,8,8192]{2,1,0:T(8,128)(2,1)S(1)} %copy-done.7, f32[1,8,8192]{2,1,0:T(8,128)S(1)} %copy-done.5, ...), kind=kLoop, calls=%fused_computation.4 | loop fusion | flops 983040 | bytes 1704000 | tf_op jit(solution)/shard_map/sub | solution.py:48
  16.7 0.2 dynamic_update_slice.13
  16.9 0.0 copy-start.1
  16.9 0.2 dynamic_update_slice.12
  17.1 0.0 copy-start
  17.1 0.2 dynamic_update_slice.11
  17.2 0.0 copy-start.3
  17.2 30.9 %all_gather.3 = bf16[65536]{0:T(1024)(128)(2,1)S(1)} all-gather(bf16[8192]{0:T(1024)(128)(2,1)S(1)} %get-tuple-element.7), channel_id=1, replica_groups=mesh['replica'=4,'fsdp'=8] {'fsdp'}, dimensions={0}, use_global_device_ids=true | all-gather | bytes 147456 | tf_op jit(solution)/shard_map/all_gather | solution.py:41
  48.1 0.7 %copy.22 = bf16[65536]{0:T(1024)(128)(2,1)} copy(bf16[65536]{0:T(1024)(128)(2,1)S(1)} %all_gather.3) | data formatting | bytes 262144
  48.8 0.0 copy-done.1
  48.8 0.0 copy-done
  48.8 0.0 copy-done.3
  (8 shorter events, 0.2 us)
Async XLA Ops:
  0.6 1.0 %copy-start.4 = (f32[8,8192]{1,0:T(8,128)S(1)}, f32[8,8192]{1,0:T(8,128)}, u32[]{:S(2)}) copy-start(f32[8,8192]{1,0:T(8,128)} %param.14) | copy-start | bytes 786436
  0.6 15.0 %copy-start.7 = (bf16[1,8,8192]{2,1,0:T(8,128)(2,1)S(1)}, bf16[1,8,8192]{2,1,0:T(8,128)(2,1)}, u32[]{:S(2)}) copy-start(bf16[1,8,8192]{2,1,0:T(8,128)(2,1)} %param.11) | copy-start | bytes 393220
  1.7 0.7 %copy-start.8 = (s32[8]{0:T(128)S(1)}, s32[8]{0:T(128)}, u32[]{:S(2)}) copy-start(s32[8]{0:T(128)} %param.8) | copy-start | bytes 100
  1.7 0.8 %copy-start.9 = (s32[8]{0:T(128)S(1)}, s32[8]{0:T(128)}, u32[]{:S(2)}) copy-start(s32[8]{0:T(128)} %param.9) | copy-start | bytes 100
  1.7 1.0 %copy-start.2 = (f32[1,8,8192]{2,1,0:T(8,128)S(1)}, f32[1,8,8192]{2,1,0:T(8,128)}, u32[]{:S(2)}) copy-start(f32[1,8,8192]{2,1,0:T(8,128)} %param.10) | copy-start | bytes 786436
  1.7 14.0 %copy-start.6 = (f32[1,8,8192]{2,1,0:T(8,128)S(1)}, f32[1,8,8192]{2,1,0:T(8,128)}, u32[]{:S(2)}) copy-start(f32[1,8,8192]{2,1,0:T(8,128)} %param.13) | copy-start | bytes 786436
  1.7 14.0 %copy-start.5 = (f32[1,8,8192]{2,1,0:T(8,128)S(1)}, f32[1,8,8192]{2,1,0:T(8,128)}, u32[]{:S(2)}) copy-start(f32[1,8,8192]{2,1,0:T(8,128)} %param.12) | copy-start | bytes 786436
  16.9 31.9 %copy-start.1 = (f32[8,8192]{1,0:T(8,128)}, f32[8,8192]{1,0:T(8,128)S(1)}, u32[]{:S(2)}) copy-start(f32[8,8192]{1,0:T(8,128)S(1)} %dynamic_update_slice.13) | copy-start | bytes 786436
  17.1 31.7 %copy-start = (f32[8,8192]{1,0:T(8,128)}, f32[8,8192]{1,0:T(8,128)S(1)}, u32[]{:S(2)}) copy-start(f32[8,8192]{1,0:T(8,128)S(1)} %dynamic_update_slice.12) | copy-start | bytes 786436
  17.2 31.5 %copy-start.3 = (f32[1,8,8192]{2,1,0:T(8,128)}, f32[1,8,8192]{2,1,0:T(8,128)S(1)}, u32[]{:S(2)}) copy-start(f32[1,8,8192]{2,1,0:T(8,128)S(1)} %dynamic_update_slice.11) | copy-start | bytes 786436
where the time goes:
time: 49 us; the launch traced here: 48.8 us
  blocking collectives  43.7 us (89%)
  local copies, waits for them, and re-layouts  3.06 us (6%)
  other arithmetic  1.08 us (2%)
  between operations  0.91 us (2%)
    all_gather x1, blocking collectives, on_device(): refreshed = lax.all_gather(refreshed_shard, 'fsdp', axis=0, tiled=True)  30.9 us
    psum x1, blocking collectives, on_device(): summed = lax.psum(drift, 'replica')  12.9 us
    unnamed x23, local copies, waits for them, and re-layouts  2.53 us
    sub x1, other arithmetic, on_device(): inner_params * (1.0 - inner_rate * decay_rate)  1.01 us

commit v1 on v0

--- a/solution.py
+++ b/solution.py
@@ -12,11 +12,44 @@
 momentum_keep = 0.9
 mix_local = 0.5
 
+AXES = ("replica", "fsdp")
+LANES = 128
+
 
 def nesterov(outer_row, moment_row, mean_drift):
     new_moment_row = momentum_keep * moment_row + mean_drift
     new_outer_row = outer_row - outer_rate * (mean_drift + momentum_keep * new_moment_row)
     return (new_outer_row, new_moment_row)
+
+
+def swap(block, replica_bits, fsdp_bits):
+    replicas, shards = lax.axis_size("replica"), lax.axis_size("fsdp")
+    pairs = [
+        (r * shards + s, (r ^ replica_bits) * shards + (s ^ fsdp_bits))
+        for r in range(replicas)
+        for s in range(shards)
+    ]
+    return lax.ppermute(block, AXES, pairs)
+
+
+def sum_over_replicas(block):
+    bit = 1
+    while bit < lax.axis_size("replica"):
+        block = block + swap(block, bit | 1, 0)
+        bit *= 2
+    return block
+
+
+def gather_over_fsdp(block):
+    shard = lax.axis_index("fsdp")
+    held = block[None]
+    bit = 1
+    while bit < lax.axis_size("fsdp"):
+        other = swap(held, 1, bit)
+        upper = (shard & bit) != 0
+        held = jnp.concatenate([jnp.where(upper, other, held), jnp.where(upper, held, other)])
+        bit *= 2
+    return held
 
 
 def on_device(
@@ -31,14 +64,19 @@
 ):
     fragment = frag_index[0]
     replicas = lax.axis_size("replica")
-    inner_row = lax.dynamic_index_in_dim(inner_params[0], fragment, 0, keepdims=False)
-    outer_row = lax.dynamic_index_in_dim(outer_params, fragment, 0, keepdims=False)
-    moment_row = lax.dynamic_index_in_dim(outer_momentum, fragment, 0, keepdims=False)
-    drift = outer_row - inner_row
-    summed = lax.psum(drift, "replica")
+    width = inner_params.shape[2]
+    tile = (width // LANES, LANES)
+
+    def row_of(table):
+        return lax.dynamic_index_in_dim(table, fragment, 0, keepdims=False).reshape(tile)
+
+    inner_row = row_of(inner_params[0])
+    outer_row = row_of(outer_params)
+    moment_row = row_of(outer_momentum)
+    summed = sum_over_replicas(outer_row - inner_row)
     new_outer_row, new_moment_row = nesterov(outer_row, moment_row, summed / replicas)
     refreshed_shard = new_outer_row.astype(jnp.bfloat16)
-    refreshed = lax.all_gather(refreshed_shard, "fsdp", axis=0, tiled=True)
+    refreshed = gather_over_fsdp(refreshed_shard).reshape(-1)
     step_count = inner_step.astype(jnp.float32)[None, :, None]
     grad_wide = grads.astype(jnp.float32)
     first_moment = beta_first * adam_first + (1.0 - beta_first) * grad_wide
@@ -49,12 +87,16 @@
         first_moment / first_fix
     ) / (jnp.sqrt(second_moment / second_fix) + adam_eps)
     stepped_row = lax.dynamic_index_in_dim(stepped, fragment, 1, keepdims=False)
-    blended = (
-        mix_local * stepped_row + (1.0 - mix_local) * refreshed_shard.astype(jnp.float32)[None, :]
+    blended = mix_local * stepped_row + (1.0 - mix_local) * refreshed_shard.astype(
+        jnp.float32
+    ).reshape(1, width)
+    new_inner = lax.dynamic_update_index_in_dim(stepped, blended, fragment, 1)
+    new_outer = lax.dynamic_update_index_in_dim(
+        outer_params, new_outer_row.reshape(width), fragment, 0
     )
-    new_inner = lax.dynamic_update_index_in_dim(stepped, blended, fragment, 1)
-    new_outer = lax.dynamic_update_index_in_dim(outer_params, new_outer_row, fragment, 0)
-    new_momentum = lax.dynamic_update_index_in_dim(outer_momentum, new_moment_row, fragment, 0)
+    new_momentum = lax.dynamic_update_index_in_dim(
+        outer_momentum, new_moment_row.reshape(width), fragment, 0
+    )
     return (new_inner, first_moment, second_moment, new_outer, new_momentum, refreshed)
 
 

time: 49 us -> 22.2 us (0.45)
  the two profiles are of different devices: /device:TPU:0 before, /device:TPU:1 now
where the time goes in v1:
time: 22.2 us; the launch traced here: 22 us
  starting transfers between devices  9.24 us (42%)
  waiting for transfers between devices  7.68 us (35%)
  local copies, waits for them, and re-layouts  2.36 us (11%)
  other arithmetic  1.84 us (8%)
  between operations  0.87 us (4%)
    ppermute x5, starting transfers between devices, swap(): return lax.ppermute(block, AXES, pairs)  9.24 us
    ppermute x5, waiting for transfers between devices, swap(): return lax.ppermute(block, AXES, pairs)  7.68 us
    unnamed x22, local copies, waits for them, and re-layouts  1.85 us
    sub x1, other arithmetic, on_device(): inner_params * (1.0 - inner_rate * decay_rate)  1.01 us
    concatenate x3, other arithmetic, gather_over_fsdp(): jnp.concatenate([jnp.where(upper, other, held), jnp.where(upper, held, ot...  0.69 us
  transfers between devices with their start and end apart: 5, of which 5 were waited for; matrix products, arithmetic and copies ran while one was open for 7% of the time, Pallas kernels for 0%

profile of v1, /device:TPU:1, one launch (start us, length us, event | category | flops | bytes accessed | tf_op | source)
XLA Modules:
  0.0 22.0 jit_solution(1607369438170009533)
XLA Ops:
  0.6 0.0 copy-start.4
  0.6 1.0 %copy.19 = f32[8,8192]{1,0:T(8,128)S(1)} copy(f32[8,8192]{1,0:T(8,128)} %param.14) | data formatting | bytes 524288
  1.6 0.0 copy-done.4
  1.7 0.0 copy-start.8
  1.7 0.7 %copy-done.8 = s32[8]{0:T(128)S(1)} copy-done((s32[8]{0:T(128)S(1)}, s32[8]{0:T(128)}, u32[]{:S(2)}) %copy-start.8) | copy-done | bytes 56
  2.5 0.0 copy-start.9
  2.5 0.1 copy-done.2
  2.7 0.1 collective-permute-start
  2.8 1.1 %collective-permute-done = f32[64,128]{1,0:T(8,128)S(1)} collective-permute-done((f32[64,128]{1,0:T(8,128)S(1)}, f32[64,128]{1,0:T(8,128)S(1)}, u32[]{:S(2)}, u32[]{:S(2)}) %collective-permute-start) | collective-permute-done | bytes 32800 | tf_op jit(solution)/shard_map/ppermute | solution.py:32
  4.0 2.6 %collective-permute-start.1 = (f32[64,128]{1,0:T(8,128)S(1)}, f32[64,128]{1,0:T(8,128)S(1)}, u32[]{:S(2)}, u32[]{:S(2)}) collective-permute-start(f32[64,128]{1,0:T(8,128)S(1)} %add.49), channel_id=1, source_target_pairs={{0,24},{1,25},{2,26},{3,27},{4,28},{5,29},{6,30},{7,31},{8,16},{9,... | collective-permute-start | bytes 98312 | tf_op jit(solution)/shard_map/ppermute | solution.py:32
  6.6 0.0 copy-done.9
  6.6 1.6 %collective-permute-done.1 = f32[64,128]{1,0:T(8,128)S(1)} collective-permute-done((f32[64,128]{1,0:T(8,128)S(1)}, f32[64,128]{1,0:T(8,128)S(1)}, u32[]{:S(2)}, u32[]{:S(2)}) %collective-permute-start.1) | collective-permute-done | bytes 32800 | tf_op jit(solution)/shard_map/ppermute | solution.py:32
  8.2 1.8 %collective-permute-start.2 = (bf16[1,64,128]{2,1,0:T(8,128)(2,1)S(1)}, bf16[1,64,128]{2,1,0:T(8,128)(2,1)S(1)}, u32[]{:S(2)}, u32[]{:S(2)}) collective-permute-start(bf16[1,64,128]{2,1,0:T(8,128)(2,1)S(1)} %get-tuple-element.6), channel_id=1, source_target_pairs={{0,9},{1,8},{2,11},{3,10},{4,13},{5,12},{6,15},{7,14},{8,1},{9,0},... | collective-permute-start | bytes 49160 | tf_op jit(solution)/shard_map/ppermute | solution.py:32
  10.0 0.0 copy-done.7
  10.0 0.0 copy-done.5
  10.0 0.0 copy-done.6
  10.0 1.0 %divide_subtract_fusion = (f32[1,8,8192]{2,1,0:T(8,128)S(1)}, f32[1,8,8192]{2,1,0:T(8,128)}, f32[1,8,8192]{2,1,0:T(8,128)}) fusion(f32[1,8,8192]{2,1,0:T(8,128)S(1)} %copy-done.2, f32[8]{0:T(128)S(1)} %get-tuple-element.19, f32[8]{0:T(128)S(1)} %get-tuple-element.18, bf16[1,8,8192]{2,1,0:T(8,128)(2,1)S(1)} %copy-done.7, f32[1,8,8192]{2,1,0:T(8,128)S(1)} %copy-done.5, ...), kind=kLoop, calls=%fused_computation.4 | loop fusion | flops 983040 | bytes 1704000 | tf_op jit(solution)/shard_map/sub | solution.py:86
  11.0 0.4 %collective-permute-done.2 = bf16[1,64,128]{2,1,0:T(8,128)(2,1)S(1)} collective-permute-done((bf16[1,64,128]{2,1,0:T(8,128)(2,1)S(1)}, bf16[1,64,128]{2,1,0:T(8,128)(2,1)S(1)}, u32[]{:S(2)}, u32[]{:S(2)}) %collective-permute-start.2) | collective-permute-done | bytes 16416 | tf_op jit(solution)/shard_map/ppermute | solution.py:32
  11.5 1.9 %collective-permute-start.3 = (bf16[2,64,128]{2,1,0:T(8,128)(2,1)S(1)}, bf16[2,64,128]{2,1,0:T(8,128)(2,1)S(1)}, u32[]{:S(2)}, u32[]{:S(2)}) collective-permute-start(bf16[2,64,128]{2,1,0:T(8,128)(2,1)S(1)} %pad_maximum_fusion.2), channel_id=1, source_target_pairs={{0,10},{1,11},{2,8},{3,9},{4,14},{5,15},{6,12},{7,13},{8,2},{9,3},... | collective-permute-start | bytes 98312 | tf_op jit(solution)/shard_map/ppermute | solution.py:32
  13.3 1.6 %collective-permute-done.3 = bf16[2,64,128]{2,1,0:T(8,128)(2,1)S(1)} collective-permute-done((bf16[2,64,128]{2,1,0:T(8,128)(2,1)S(1)}, bf16[2,64,128]{2,1,0:T(8,128)(2,1)S(1)}, u32[]{:S(2)}, u32[]{:S(2)}) %collective-permute-start.3) | collective-permute-done | bytes 32800 | tf_op jit(solution)/shard_map/ppermute | solution.py:32
  14.9 2.8 %collective-permute-start.4 = (bf16[4,64,128]{2,1,0:T(8,128)(2,1)S(1)}, bf16[4,64,128]{2,1,0:T(8,128)(2,1)S(1)}, u32[]{:S(2)}, u32[]{:S(2)}) collective-permute-start(bf16[4,64,128]{2,1,0:T(8,128)(2,1)S(1)} %pad_maximum_fusion.1), channel_id=1, source_target_pairs={{0,12},{1,13},{2,14},{3,15},{4,8},{5,9},{6,10},{7,11},{8,4},{9,5},... | collective-permute-start | bytes 196616 | tf_op jit(solution)/shard_map/ppermute | solution.py:32
  17.8 0.2 dynamic_update_slice.11
  18.0 0.0 copy-start.3
  18.0 0.2 dynamic_update_slice.12
  18.1 0.0 copy-start.1
  18.1 0.2 dynamic_update_slice.13
  18.3 0.0 copy-start
  18.3 3.0 %collective-permute-done.4 = bf16[4,64,128]{2,1,0:T(8,128)(2,1)S(1)} collective-permute-done((bf16[4,64,128]{2,1,0:T(8,128)(2,1)S(1)}, bf16[4,64,128]{2,1,0:T(8,128)(2,1)S(1)}, u32[]{:S(2)}, u32[]{:S(2)}) %collective-permute-start.4) | collective-permute-done | bytes 65568 | tf_op jit(solution)/shard_map/ppermute | solution.py:32
  21.3 0.7 %pad_maximum_fusion = bf16[8,64,128]{2,1,0:T(8,128)(2,1)} fusion(bf16[4,64,128]{2,1,0:T(8,128)(2,1)S(1)} %get-tuple-element.12, bf16[4,64,128]{2,1,0:T(8,128)(2,1)S(1)} %get-tuple-element.11), kind=kLoop, calls=%fused_computation.5 | loop fusion | flops 65536 | bytes 262144 | tf_op jit(solution)/shard_map/concatenate | solution.py:50
  22.0 0.0 copy-done.1
  22.0 0.0 copy-done
  22.0 0.0 copy-done.3
  (19 shorter events, 0.2 us)
Async XLA Ops:
  0.6 1.0 %copy-start.4 = (f32[8,8192]{1,0:T(8,128)S(1)}, f32[8,8192]{1,0:T(8,128)}, u32[]{:S(2)}) copy-start(f32[8,8192]{1,0:T(8,128)} %param.15) | copy-start | bytes 786436
  1.7 1.0 %copy-start.2 = (f32[1,8,8192]{2,1,0:T(8,128)S(1)}, f32[1,8,8192]{2,1,0:T(8,128)}, u32[]{:S(2)}) copy-start(f32[1,8,8192]{2,1,0:T(8,128)} %param.10) | copy-start | bytes 786436
  1.7 8.4 %copy-start.7 = (bf16[1,8,8192]{2,1,0:T(8,128)(2,1)S(1)}, bf16[1,8,8192]{2,1,0:T(8,128)(2,1)}, u32[]{:S(2)}) copy-start(bf16[1,8,8192]{2,1,0:T(8,128)(2,1)} %param.11) | copy-start | bytes 393220
  1.7 0.7 %copy-start.8 = (s32[8]{0:T(128)S(1)}, s32[8]{0:T(128)}, u32[]{:S(2)}) copy-start(s32[8]{0:T(128)} %param.8) | copy-start | bytes 100
  2.5 4.1 %copy-start.9 = (s32[8]{0:T(128)S(1)}, s32[8]{0:T(128)}, u32[]{:S(2)}) copy-start(s32[8]{0:T(128)} %param.9) | copy-start | bytes 100
  2.6 7.4 %copy-start.5 = (f32[1,8,8192]{2,1,0:T(8,128)S(1)}, f32[1,8,8192]{2,1,0:T(8,128)}, u32[]{:S(2)}) copy-start(f32[1,8,8192]{2,1,0:T(8,128)} %param.12) | copy-start | bytes 786436
  2.6 7.4 %copy-start.6 = (f32[1,8,8192]{2,1,0:T(8,128)S(1)}, f32[1,8,8192]{2,1,0:T(8,128)}, u32[]{:S(2)}) copy-start(f32[1,8,8192]{2,1,0:T(8,128)} %param.13) | copy-start | bytes 786436
  2.7 1.3 %collective-permute-start = (f32[64,128]{1,0:T(8,128)S(1)}, f32[64,128]{1,0:T(8,128)S(1)}, u32[]{:S(2)}, u32[]{:S(2)}) collective-permute-start(f32[64,128]{1,0:T(8,128)S(1)} %sub.20), channel_id=1, source_target_pairs={{0,8},{1,9},{2,10},{3,11},{4,12},{5,13},{6,14},{7,15},{8,0},{9,1},... | collective-permute-start | bytes 98312 | tf_op jit(solution)/shard_map/ppermute | solution.py:32
  4.0 4.2 %collective-permute-start.1 = (f32[64,128]{1,0:T(8,128)S(1)}, f32[64,128]{1,0:T(8,128)S(1)}, u32[]{:S(2)}, u32[]{:S(2)}) collective-permute-start(f32[64,128]{1,0:T(8,128)S(1)} %add.49), channel_id=1, source_target_pairs={{0,24},{1,25},{2,26},{3,27},{4,28},{5,29},{6,30},{7,31},{8,16},{9,... | collective-permute-start | bytes 98312 | tf_op jit(solution)/shard_map/ppermute | solution.py:32
  8.2 3.3 %collective-permute-start.2 = (bf16[1,64,128]{2,1,0:T(8,128)(2,1)S(1)}, bf16[1,64,128]{2,1,0:T(8,128)(2,1)S(1)}, u32[]{:S(2)}, u32[]{:S(2)}) collective-permute-start(bf16[1,64,128]{2,1,0:T(8,128)(2,1)S(1)} %get-tuple-element.6), channel_id=1, source_target_pairs={{0,9},{1,8},{2,11},{3,10},{4,13},{5,12},{6,15},{7,14},{8,1},{9,0},... | collective-permute-start | bytes 49160 | tf_op jit(solution)/shard_map/ppermute | solution.py:32
  11.5 3.5 %collective-permute-start.3 = (bf16[2,64,128]{2,1,0:T(8,128)(2,1)S(1)}, bf16[2,64,128]{2,1,0:T(8,128)(2,1)S(1)}, u32[]{:S(2)}, u32[]{:S(2)}) collective-permute-start(bf16[2,64,128]{2,1,0:T(8,128)(2,1)S(1)} %pad_maximum_fusion.2), channel_id=1, source_target_pairs={{0,10},{1,11},{2,8},{3,9},{4,14},{5,15},{6,12},{7,13},{8,2},{9,3},... | collective-permute-start | bytes 98312 | tf_op jit(solution)/shard_map/ppermute | solution.py:32
  14.9 6.4 %collective-permute-start.4 = (bf16[4,64,128]{2,1,0:T(8,128)(2,1)S(1)}, bf16[4,64,128]{2,1,0:T(8,128)(2,1)S(1)}, u32[]{:S(2)}, u32[]{:S(2)}) collective-permute-start(bf16[4,64,128]{2,1,0:T(8,128)(2,1)S(1)} %pad_maximum_fusion.1), channel_id=1, source_target_pairs={{0,12},{1,13},{2,14},{3,15},{4,8},{5,9},{6,10},{7,11},{8,4},{9,5},... | collective-permute-start | bytes 196616 | tf_op jit(solution)/shard_map/ppermute | solution.py:32
  18.0 4.0 %copy-start.3 = (f32[1,8,8192]{2,1,0:T(8,128)}, f32[1,8,8192]{2,1,0:T(8,128)S(1)}, u32[]{:S(2)}) copy-start(f32[1,8,8192]{2,1,0:T(8,128)S(1)} %dynamic_update_slice.11) | copy-start | bytes 786436
  18.1 3.9 %copy-start.1 = (f32[8,8192]{1,0:T(8,128)}, f32[8,8192]{1,0:T(8,128)S(1)}, u32[]{:S(2)}) copy-start(f32[8,8192]{1,0:T(8,128)S(1)} %dynamic_update_slice.12) | copy-start | bytes 786436
  18.3 3.7 %copy-start = (f32[8,8192]{1,0:T(8,128)}, f32[8,8192]{1,0:T(8,128)S(1)}, u32[]{:S(2)}) copy-start(f32[8,8192]{1,0:T(8,128)S(1)} %dynamic_update_slice.13) | copy-start | bytes 786436

commit v2 on v0

v2 whole, which is shorter than its diff:
```python
import jax
import jax.numpy as jnp
from jax import lax
from jax.experimental import pallas as pl
from jax.experimental.pallas import tpu as pltpu
from jax.sharding import PartitionSpec as P

beta_first = 0.9
beta_second = 0.95
adam_eps = 1e-08
inner_rate = 0.05
decay_rate = 0.1
outer_rate = 0.7
momentum_keep = 0.9
mix_local = 0.5

AXES = ("replica", "fsdp")
LANES = 128
SUBLANES = 8


def nesterov(outer_row, moment_row, mean_drift):
    new_moment_row = momentum_keep * moment_row + mean_drift
    new_outer_row = outer_row - outer_rate * (mean_drift + momentum_keep * new_moment_row)
    return (new_outer_row, new_moment_row)


def begin_kernel(
    index_hbm, inner_hbm, outer_hbm, moment_hbm, drift, outer, moment, index, inner, sems
):
    sources = (index_hbm, inner_hbm.at[0], outer_hbm, moment_hbm)
    targets = (index, inner, outer, moment)
    copies = [
        pltpu.make_async_copy(source, target, sems.at[i])
        for i, (source, target) in enumerate(zip(sources, targets))
    ]
    for copy in copies:
        copy.start()
    for copy in copies[:3]:
        copy.wait()
    fragment = index[0]
    sublane = lax.broadcasted_iota(jnp.int32, (SUBLANES, LANES), 0)
    for top in range(0, drift.shape[0], SUBLANES):
        folded = jnp.zeros((SUBLANES, LANES), jnp.float32)
        for i in range(SUBLANES):
            columns = pl.ds((top + i) * LANES, LANES)
            every = outer[:, columns] - inner[:, columns]
            turned = pltpu.roll(every, (i + SUBLANES - fragment) % SUBLANES, 0)
            folded = jnp.where(sublane == i, turned, folded)
        drift[pl.ds(top, SUBLANES), :] = folded
    copies[3].wait()


def begin(frag_index, inner_params, outer_params, outer_momentum):
    frags, width = outer_params.shape
    return pl.pallas_call(
        begin_kernel,
        out_shape=(
            pltpu.VMEM((width // LANES, LANES), jnp.float32),
            pltpu.VMEM((frags, width), jnp.float32),
            pltpu.VMEM((frags, width), jnp.float32),
        ),
        in_specs=[pl.BlockSpec(memory_space=pl.ANY)] * 4,
        out_specs=[pl.BlockSpec(memory_space=pltpu.VMEM)] * 3,
        scratch_shapes=[
            pltpu.SMEM(frag_index.shape, jnp.int32),
            pltpu.VMEM((frags, width), jnp.float32),
            pltpu.SemaphoreType.DMA((4,)),
        ],
        name="begin",
    )(frag_index, inner_params, outer_params, outer_momentum)


def swap(block, replica_bits, fsdp_bits):
    replicas, shards = lax.axis_size("replica"), lax.axis_size("fsdp")
    pairs = [
        (r * shards + s, (r ^ replica_bits) * shards + (s ^ fsdp_bits))
        for r in range(replicas)
        for s in range(shards)
    ]
    return lax.ppermute(block, AXES, pairs)


def after(arrays, earlier):
    return lax.optimization_barrier((tuple(arrays), earlier))[0]


def gather_upper(block):
    shard = lax.axis_index("fsdp")
    held = block[None]
    bit = lax.axis_size("fsdp") // 2
    while bit > 2:
        other = swap(held, 1, bit)
        upper = (shard & bit) != 0
        held = jnp.stack(
            [jnp.where(upper, other, held), jnp.where(upper, held, other)], axis=1
        ).reshape(-1, *block.shape)
        bit //= 2
    return held


def gather_lower(held):
    shard = lax.axis_index("fsdp")
    first, second, both = (swap(held, 1, bits) for bits in (1, 2, 3))
    even, odd, low = (shard & 1) == 0, (shard & 1) != 0, (shard & 2) == 0
    near = (jnp.where(even, held, first), jnp.where(even, first, held))
    far = (jnp.where(odd, both, second), jnp.where(odd, second, both))
    lower = [jnp.where(low, n, f) for n, f in zip(near, far)]
    upper = [jnp.where(low, f, n) for n, f in zip(near, far)]
    return jnp.stack(lower + upper, axis=1)


def on_device(
    frag_index,
    inner_step,
    inner_params,
    grads,
    adam_first,
    adam_second,
    outer_params,
    outer_momentum,
):
    fragment = frag_index[0]
    replicas = lax.axis_size("replica")
    frags, width = outer_params.shape
    chosen = (jnp.arange(frags) == fragment)[:, None]

    def row_of(table):
        row = lax.dynamic_index_in_dim(table, fragment, 0, keepdims=False)
        return row.reshape(width // LANES, LANES)

    def put_row(row, table):
        return jnp.where(chosen, row.reshape(1, width), table)

    drift, outer_params, outer_momentum = begin(
        frag_index, inner_params, outer_params, outer_momentum
    )
    summed = drift + swap(drift, 1, 0)
    inner_params, grads, adam_first, adam_second = after(
        (inner_params, grads, adam_first, adam_second), summed
    )
    bit = 2
    while bit < replicas:
        summed = summed + swap(summed, bit | 1, 0)
        bit *= 2

    step_count = inner_step.astype(jnp.float32)[None, :, None]
    grad_wide = grads.astype(jnp.float32)
    first_moment = beta_first * adam_first + (1.0 - beta_first) * grad_wide
    second_moment = beta_second * adam_second + (1.0 - beta_second) * grad_wide * grad_wide
    first_fix = 1.0 - jnp.power(jnp.float32(beta_first), step_count)
    second_fix = 1.0 - jnp.power(jnp.float32(beta_second), step_count)
    stepped = inner_params * (1.0 - inner_rate * decay_rate) - inner_rate * (
        first_moment / first_fix
    ) / (jnp.sqrt(second_moment / second_fix) + adam_eps)

    outer_row, moment_row = row_of(outer_params), row_of(outer_momentum)
    new_outer_row, new_moment_row = nesterov(outer_row, moment_row, summed / replicas)
    refreshed_shard = new_outer_row.astype(jnp.bfloat16)
    held = gather_upper(refreshed_shard)
    new_outer = put_row(new_outer_row, outer_params)
    new_momentum = put_row(new_moment_row, outer_momentum)
    refreshed = gather_lower(held).reshape(-1)
    stepped, refreshed_shard = after((stepped, refreshed_shard), held)
    refreshed_row = refreshed_shard.astype(jnp.float32).reshape(1, 1, width)
    blended = mix_local * stepped + (1.0 - mix_local) * refreshed_row
    new_inner = jnp.where(chosen[None], blended, stepped)
    return (new_inner, first_moment, second_moment, new_outer, new_momentum, refreshed)


def solution(mesh):
    return jax.shard_map(
        on_device,
        mesh=mesh,
        in_specs=(
            P(),
            P(),
            P("replica", None, "fsdp"),
            P("replica", None, "fsdp"),
            P("replica", None, "fsdp"),
            P("replica", None, "fsdp"),
            P(None, "fsdp"),
            P(None, "fsdp"),
        ),
        out_specs=(
            P("replica", None, "fsdp"),
            P("replica", None, "fsdp"),
            P("replica", None, "fsdp"),
            P(None, "fsdp"),
            P(None, "fsdp"),
            P(),
        ),
        check_vma=False,
    )
```

time: 49 us -> 19.1 us (0.39)
  blocking collectives: 43.7 us -> 0 us
  starting transfers between devices: 0 us -> 9.25 us
  waiting for transfers between devices: 0 us -> 4.04 us
  local copies, waits for them, and re-layouts: 3.06 us -> 0.69 us
  other arithmetic: 1.08 us -> 2.9 us
  Pallas kernels: 0 us -> 1.21 us
    all_gather x1 -> x0, blocking collectives: 30.9 us -> none  [on_device(): refreshed = lax.all_gather(refreshed_shard, 'fsdp', axis=0, tiled=True)]
    psum x1 -> x0, blocking collectives: 12.9 us -> none  [on_device(): summed = lax.psum(drift, 'replica')]
    ppermute x0 -> x6, starting transfers between devices: none -> 9.25 us  [swap(): return lax.ppermute(block, AXES, pairs)]
    ppermute x0 -> x6, waiting for transfers between devices: none -> 4.04 us  [swap(): return lax.ppermute(block, AXES, pairs)]
    unnamed x23 -> x12, local copies, waits for them, and re-layouts: 2.53 us -> 0.03 us
    select_n x0 -> x2, other arithmetic: none -> 1.7 us  [the longest x1 0.91 us: put_row(): return jnp.where(chosen, row.reshape(1, width), table)]
    pallas_call x0 -> x1, Pallas kernels: none -> 1.21 us  [begin(): pl.pallas_call(begin_kernel, out_shape=(pltpu.VMEM((width // LANES, LANES...]
    another operation x0 -> x1, local copies, waits for them, and re-layouts: none -> 0.66 us  [gather_lower(): return jnp.stack(lower + upper, axis=1)]
  transfers between devices with their start and end apart: 0 -> 6, of which waited for: 0 -> 6; matrix products, arithmetic and copies ran while one was open for 0% -> 15% of each run, Pallas kernels for 0% -> 0%
where the time goes in v2:
time: 19.1 us; the launch traced here: 19 us
  starting transfers between devices  9.25 us (48%)
  waiting for transfers between devices  4.04 us (21%)
  other arithmetic  2.9 us (15%)
  Pallas kernels  1.21 us (6%)
  between operations  0.88 us (5%)
  local copies, waits for them, and re-layouts  0.69 us (4%)
    ppermute x6, starting transfers between devices, swap(): return lax.ppermute(block, AXES, pairs)  9.25 us
    ppermute x6, waiting for transfers between devices, swap(): return lax.ppermute(block, AXES, pairs)  4.04 us
    pallas_call x1, Pallas kernels, begin(): pl.pallas_call(begin_kernel, out_shape=(pltpu.VMEM((width // LANES, LANES...  1.21 us
    sub x1, other arithmetic, on_device(): inner_params * (1.0 - inner_rate * decay_rate)  1.01 us
    select_n x1, other arithmetic, put_row(): return jnp.where(chosen, row.reshape(1, width), table)  0.91 us
    select_n x1, other arithmetic, on_device(): new_inner = jnp.where(chosen[None], blended, stepped)  0.79 us
    another operation x1, local copies, waits for them, and re-layouts, gather_lower(): return jnp.stack(lower + upper, axis=1)  0.66 us
  transfers between devices with their start and end apart: 6, of which 6 were waited for; matrix products, arithmetic and copies ran while one was open for 15% of the time, Pallas kernels for 0%

profile of v2, /device:TPU:0, one launch (start us, length us, event | category | flops | bytes accessed | tf_op | source)
XLA Modules:
  0.0 19.0 jit_solution(16375626770931825813)
XLA Ops:
  0.6 0.0 copy-start.4
  0.6 0.0 copy-start.5
  0.7 0.0 copy-start.1
  0.7 0.0 copy-start.2
  0.7 0.0 copy-start.3
  0.7 1.2 %begin.1 = (f32[64,128]{1,0:T(8,128)S(1)}, f32[8,8192]{1,0:T(8,128)S(1)}, f32[8,8192]{1,0:T(8,128)S(1)}) custom-call(s32[8]{0:T(128)} %index_hbm.1, f32[1,8,8192]{2,1,0:T(8,128)} %inner_hbm.1, f32[8,8192]{1,0:T(8,128)} %outer_hbm.1, f32[8,8192]{1,0:T(8,128)} %moment_hbm.1), custom_call_target="tpu_custom_call" | custom-call | tf_op jit(solution)/shard_map/begin/pallas_call | solution.py:56
  1.9 0.0 copy-start
  1.9 0.5 %collective-permute-start = (f32[64,128]{1,0:T(8,128)S(1)}, f32[64,128]{1,0:T(8,128)S(1)}, u32[]{:S(2)}, u32[]{:S(2)}) collective-permute-start(f32[64,128]{1,0:T(8,128)S(1)} %get-tuple-element.15), channel_id=1, source_target_pairs={{0,8},{1,9},{2,10},{3,11},{4,12},{5,13},{6,14},{7,15},{8,0},{9,1},... | collective-permute-start | bytes 98312 | tf_op jit(solution)/shard_map/ppermute | solution.py:81
  2.4 0.0 copy-done.4
  2.5 0.0 copy-done.5
  2.6 0.1 dynamic-slice_multiply_fusion
  2.7 0.6 %collective-permute-done = f32[64,128]{1,0:T(8,128)S(1)} collective-permute-done((f32[64,128]{1,0:T(8,128)S(1)}, f32[64,128]{1,0:T(8,128)S(1)}, u32[]{:S(2)}, u32[]{:S(2)}) %collective-permute-start) | collective-permute-done | bytes 32800 | tf_op jit(solution)/shard_map/ppermute | solution.py:81
  3.3 2.6 %collective-permute-start.1 = (f32[64,128]{1,0:T(8,128)S(1)}, f32[64,128]{1,0:T(8,128)S(1)}, u32[]{:S(2)}, u32[]{:S(2)}) collective-permute-start(f32[64,128]{1,0:T(8,128)S(1)} %add.37), channel_id=1, source_target_pairs={{0,24},{1,25},{2,26},{3,27},{4,28},{5,29},{6,30},{7,31},{8,16},{9,... | collective-permute-start | bytes 98312 | tf_op jit(solution)/shard_map/ppermute | solution.py:81
  5.9 0.0 copy-done.1
  5.9 0.0 copy-done.2
  5.9 0.0 copy-done.3
  5.9 0.0 copy-done
  5.9 1.0 %divide_subtract_fusion = (f32[1,8,8192]{2,1,0:T(8,128)S(1)}, f32[1,8,8192]{2,1,0:T(8,128)}, f32[1,8,8192]{2,1,0:T(8,128)}) fusion(f32[1,8,8192]{2,1,0:T(8,128)S(1)} %copy-done, f32[8]{0:T(128)S(1)} %get-tuple-element.39, f32[8]{0:T(128)S(1)} %get-tuple-element.38, bf16[1,8,8192]{2,1,0:T(8,128)(2,1)S(1)} %copy-done.3, f32[1,8,8192]{2,1,0:T(8,128)S(1)} %copy-done.1, ...), kind=kLoop, calls=%fused_computation.5 | loop fusion | flops 983040 | bytes 1704000 | tf_op jit(solution)/shard_map/sub | solution.py:153
  6.9 0.6 %collective-permute-done.1 = f32[64,128]{1,0:T(8,128)S(1)} collective-permute-done((f32[64,128]{1,0:T(8,128)S(1)}, f32[64,128]{1,0:T(8,128)S(1)}, u32[]{:S(2)}, u32[]{:S(2)}) %collective-permute-start.1) | collective-permute-done | bytes 32800 | tf_op jit(solution)/shard_map/ppermute | solution.py:81
  7.5 2.9 %collective-permute-start.2 = (bf16[1,64,128]{2,1,0:T(8,128)(2,1)S(1)}, bf16[1,64,128]{2,1,0:T(8,128)(2,1)S(1)}, u32[]{:S(2)}, u32[]{:S(2)}) collective-permute-start(bf16[1,64,128]{2,1,0:T(8,128)(2,1)S(1)} %bitcast.35), channel_id=1, source_target_pairs={{0,12},{1,13},{2,14},{3,15},{4,8},{5,9},{6,10},{7,11},{8,4},{9,5},... | collective-permute-start | bytes 49160 | tf_op jit(solution)/shard_map/ppermute | solution.py:81
  10.4 0.9 %broadcast_select_fusion = (f32[8,8192]{1,0:T(8,128)}, f32[8,8192]{1,0:T(8,128)}) fusion(f32[8,8192]{1,0:T(8,128)S(1)} %get-tuple-element.21, f32[8192]{0:T(1024)S(1)} %get-tuple-element.33, pred[8]{0:T(512)(128)(4,1)S(1)} %iota_compare_fusion, f32[8,8192]{1,0:T(8,128)S(1)} %get-tuple-element.20, f32[8192]{0:T(1024)S(1)} %bitcast.37), kind=kLoop, calls=%fused_computation.7 | loop fusion | flops 131072 | bytes 1114120 | tf_op jit(solution)/shard_map/jit(_where)/select_n | solution.py:133
  11.3 0.5 %collective-permute-done.2 = bf16[1,64,128]{2,1,0:T(8,128)(2,1)S(1)} collective-permute-done((bf16[1,64,128]{2,1,0:T(8,128)(2,1)S(1)}, bf16[1,64,128]{2,1,0:T(8,128)(2,1)S(1)}, u32[]{:S(2)}, u32[]{:S(2)}) %collective-permute-start.2) | collective-permute-done | bytes 16416 | tf_op jit(solution)/shard_map/ppermute | solution.py:81
  11.9 2.6 %collective-permute-start.4 = (bf16[2,64,128]{2,1,0:T(8,128)(2,1)S(1)}, bf16[2,64,128]{2,1,0:T(8,128)(2,1)S(1)}, u32[]{:S(2)}, u32[]{:S(2)}) collective-permute-start(bf16[2,64,128]{2,1,0:T(8,128)(2,1)S(1)} %maximum_bitcast_fusion), channel_id=1, source_target_pairs={{0,11},{1,10},{2,9},{3,8},{4,15},{5,14},{6,13},{7,12},{8,3},{9,2},... | collective-permute-start | bytes 98312 | tf_op jit(solution)/shard_map/ppermute | solution.py:81
  14.5 0.4 %collective-permute-start.5 = (bf16[2,64,128]{2,1,0:T(8,128)(2,1)S(1)}, bf16[2,64,128]{2,1,0:T(8,128)(2,1)S(1)}, u32[]{:S(2)}, u32[]{:S(2)}) collective-permute-start(bf16[2,64,128]{2,1,0:T(8,128)(2,1)S(1)} %maximum_bitcast_fusion), channel_id=1, source_target_pairs={{0,10},{1,11},{2,8},{3,9},{4,14},{5,15},{6,12},{7,13},{8,2},{9,3},... | collective-permute-start | bytes 98312 | tf_op jit(solution)/shard_map/ppermute | solution.py:81
  14.9 0.2 %collective-permute-start.3 = (bf16[2,64,128]{2,1,0:T(8,128)(2,1)S(1)}, bf16[2,64,128]{2,1,0:T(8,128)(2,1)S(1)}, u32[]{:S(2)}, u32[]{:S(2)}) collective-permute-start(bf16[2,64,128]{2,1,0:T(8,128)(2,1)S(1)} %maximum_bitcast_fusion), channel_id=1, source_target_pairs={{0,9},{1,8},{2,11},{3,10},{4,13},{5,12},{6,15},{7,14},{8,1},{9,0},... | collective-permute-start | bytes 98312 | tf_op jit(solution)/shard_map/ppermute | solution.py:81
  15.1 0.8 %add_select_fusion = f32[1,8,8192]{2,1,0:T(8,128)} fusion(f32[1,8,8192]{2,1,0:T(8,128)S(1)} %get-tuple-element.22, f32[8192]{0:T(1024)S(1)} %multiply_bitcast_fusion, pred[8]{0:T(512)(128)(4,1)S(1)} %iota_compare_fusion), kind=kLoop, calls=%fused_computation.4 | loop fusion | flops 196608 | bytes 557064 | tf_op jit(solution)/shard_map/jit(_where)/select_n | solution.py:167
  15.9 0.3 %collective-permute-done.4 = bf16[2,64,128]{2,1,0:T(8,128)(2,1)S(1)} collective-permute-done((bf16[2,64,128]{2,1,0:T(8,128)(2,1)S(1)}, bf16[2,64,128]{2,1,0:T(8,128)(2,1)S(1)}, u32[]{:S(2)}, u32[]{:S(2)}) %collective-permute-start.4) | collective-permute-done | bytes 32800 | tf_op jit(solution)/shard_map/ppermute | solution.py:81
  16.2 1.6 %collective-permute-done.5 = bf16[2,64,128]{2,1,0:T(8,128)(2,1)S(1)} collective-permute-done((bf16[2,64,128]{2,1,0:T(8,128)(2,1)S(1)}, bf16[2,64,128]{2,1,0:T(8,128)(2,1)S(1)}, u32[]{:S(2)}, u32[]{:S(2)}) %collective-permute-start.5) | collective-permute-done | bytes 32800 | tf_op jit(solution)/shard_map/ppermute | solution.py:81
  17.9 0.4 %collective-permute-done.3 = bf16[2,64,128]{2,1,0:T(8,128)(2,1)S(1)} collective-permute-done((bf16[2,64,128]{2,1,0:T(8,128)(2,1)S(1)}, bf16[2,64,128]{2,1,0:T(8,128)(2,1)S(1)}, u32[]{:S(2)}, u32[]{:S(2)}) %collective-permute-start.3) | collective-permute-done | bytes 32800 | tf_op jit(solution)/shard_map/ppermute | solution.py:81
  18.3 0.7 %copy.14 = bf16[2,4,64,128]{3,2,1,0:T(8,128)(2,1)} copy(bf16[2,4,64,128]{3,2,0,1:T(8,128)(2,1)S(1)} %pad_maximum_fusion) | data formatting | bytes 262144 | tf_op jit(solution)/shard_map/stack | solution.py:110
  (9 shorter events, 0.1 us)
Async XLA Ops:
  0.6 1.8 %copy-start.4 = (s32[8]{0:T(128)S(1)}, s32[8]{0:T(128)}, u32[]{:S(2)}) copy-start(s32[8]{0:T(128)} %index_hbm.1) | copy-start | bytes 100
  0.6 1.9 %copy-start.5 = (s32[8]{0:T(128)S(1)}, s32[8]{0:T(128)}, u32[]{:S(2)}) copy-start(s32[8]{0:T(128)} %param.9) | copy-start | bytes 100
  0.7 5.2 %copy-start.1 = (f32[1,8,8192]{2,1,0:T(8,128)S(1)}, f32[1,8,8192]{2,1,0:T(8,128)}, u32[]{:S(2)}) copy-start(f32[1,8,8192]{2,1,0:T(8,128)} %param.12) | copy-start | bytes 786436
  0.7 5.2 %copy-start.2 = (f32[1,8,8192]{2,1,0:T(8,128)S(1)}, f32[1,8,8192]{2,1,0:T(8,128)}, u32[]{:S(2)}) copy-start(f32[1,8,8192]{2,1,0:T(8,128)} %param.13) | copy-start | bytes 786436
  0.7 5.2 %copy-start.3 = (bf16[1,8,8192]{2,1,0:T(8,128)(2,1)S(1)}, bf16[1,8,8192]{2,1,0:T(8,128)(2,1)}, u32[]{:S(2)}) copy-start(bf16[1,8,8192]{2,1,0:T(8,128)(2,1)} %param.11) | copy-start | bytes 393220
  1.9 4.0 %copy-start = (f32[1,8,8192]{2,1,0:T(8,128)S(1)}, f32[1,8,8192]{2,1,0:T(8,128)}, u32[]{:S(2)}) copy-start(f32[1,8,8192]{2,1,0:T(8,128)} %inner_hbm.1) | copy-start | bytes 786436
  1.9 1.4 %collective-permute-start = (f32[64,128]{1,0:T(8,128)S(1)}, f32[64,128]{1,0:T(8,128)S(1)}, u32[]{:S(2)}, u32[]{:S(2)}) collective-permute-start(f32[64,128]{1,0:T(8,128)S(1)} %get-tuple-element.15), channel_id=1, source_target_pairs={{0,8},{1,9},{2,10},{3,11},{4,12},{5,13},{6,14},{7,15},{8,0},{9,1},... | collective-permute-start | bytes 98312 | tf_op jit(solution)/shard_map/ppermute | solution.py:81
  3.3 4.2 %collective-permute-start.1 = (f32[64,128]{1,0:T(8,128)S(1)}, f32[64,128]{1,0:T(8,128)S(1)}, u32[]{:S(2)}, u32[]{:S(2)}) collective-permute-start(f32[64,128]{1,0:T(8,128)S(1)} %add.37), channel_id=1, source_target_pairs={{0,24},{1,25},{2,26},{3,27},{4,28},{5,29},{6,30},{7,31},{8,16},{9,... | collective-permute-start | bytes 98312 | tf_op jit(solution)/shard_map/ppermute | solution.py:81
  7.5 4.4 %collective-permute-start.2 = (bf16[1,64,128]{2,1,0:T(8,128)(2,1)S(1)}, bf16[1,64,128]{2,1,0:T(8,128)(2,1)S(1)}, u32[]{:S(2)}, u32[]{:S(2)}) collective-permute-start(bf16[1,64,128]{2,1,0:T(8,128)(2,1)S(1)} %bitcast.35), channel_id=1, source_target_pairs={{0,12},{1,13},{2,14},{3,15},{4,8},{5,9},{6,10},{7,11},{8,4},{9,5},... | collective-permute-start | bytes 49160 | tf_op jit(solution)/shard_map/ppermute | solution.py:81
  11.9 4.3 %collective-permute-start.4 = (bf16[2,64,128]{2,1,0:T(8,128)(2,1)S(1)}, bf16[2,64,128]{2,1,0:T(8,128)(2,1)S(1)}, u32[]{:S(2)}, u32[]{:S(2)}) collective-permute-start(bf16[2,64,128]{2,1,0:T(8,128)(2,1)S(1)} %maximum_bitcast_fusion), channel_id=1, source_target_pairs={{0,11},{1,10},{2,9},{3,8},{4,15},{5,14},{6,13},{7,12},{8,3},{9,2},... | collective-permute-start | bytes 98312 | tf_op jit(solution)/shard_map/ppermute | solution.py:81
  14.5 3.3 %collective-permute-start.5 = (bf16[2,64,128]{2,1,0:T(8,128)(2,1)S(1)}, bf16[2,64,128]{2,1,0:T(8,128)(2,1)S(1)}, u32[]{:S(2)}, u32[]{:S(2)}) collective-permute-start(bf16[2,64,128]{2,1,0:T(8,128)(2,1)S(1)} %maximum_bitcast_fusion), channel_id=1, source_target_pairs={{0,10},{1,11},{2,8},{3,9},{4,14},{5,15},{6,12},{7,13},{8,2},{9,3},... | collective-permute-start | bytes 98312 | tf_op jit(solution)/shard_map/ppermute | solution.py:81
  14.9 3.3 %collective-permute-start.3 = (bf16[2,64,128]{2,1,0:T(8,128)(2,1)S(1)}, bf16[2,64,128]{2,1,0:T(8,128)(2,1)S(1)}, u32[]{:S(2)}, u32[]{:S(2)}) collective-permute-start(bf16[2,64,128]{2,1,0:T(8,128)(2,1)S(1)} %maximum_bitcast_fusion), channel_id=1, source_target_pairs={{0,9},{1,8},{2,11},{3,10},{4,13},{5,12},{6,15},{7,14},{8,1},{9,0},... | collective-permute-start | bytes 98312 | tf_op jit(solution)/shard_map/ppermute | solution.py:81

commit v3 on v2

--- a/solution.py
+++ b/solution.py
@@ -25,50 +25,65 @@
     return (new_outer_row, new_moment_row)
 
 
-def begin_kernel(
-    index_hbm, inner_hbm, outer_hbm, moment_hbm, drift, outer, moment, index, inner, sems
-):
-    sources = (index_hbm, inner_hbm.at[0], outer_hbm, moment_hbm)
-    targets = (index, inner, outer, moment)
+def begin_kernel(*refs):
+    sources, targets, sems = refs[:4], refs[4:8], refs[8]
     copies = [
         pltpu.make_async_copy(source, target, sems.at[i])
         for i, (source, target) in enumerate(zip(sources, targets))
     ]
     for copy in copies:
         copy.start()
-    for copy in copies[:3]:
+    for copy in copies:
         copy.wait()
-    fragment = index[0]
-    sublane = lax.broadcasted_iota(jnp.int32, (SUBLANES, LANES), 0)
-    for top in range(0, drift.shape[0], SUBLANES):
-        folded = jnp.zeros((SUBLANES, LANES), jnp.float32)
-        for i in range(SUBLANES):
-            columns = pl.ds((top + i) * LANES, LANES)
-            every = outer[:, columns] - inner[:, columns]
-            turned = pltpu.roll(every, (i + SUBLANES - fragment) % SUBLANES, 0)
-            folded = jnp.where(sublane == i, turned, folded)
-        drift[pl.ds(top, SUBLANES), :] = folded
-    copies[3].wait()
-
-
-def begin(frag_index, inner_params, outer_params, outer_momentum):
-    frags, width = outer_params.shape
+
+
+def begin(*arrays):
+    memories = (pltpu.SMEM,) + (pltpu.VMEM,) * 3
     return pl.pallas_call(
         begin_kernel,
-        out_shape=(
-            pltpu.VMEM((width // LANES, LANES), jnp.float32),
-            pltpu.VMEM((frags, width), jnp.float32),
-            pltpu.VMEM((frags, width), jnp.float32),
-        ),
+        out_shape=[memory(x.shape, x.dtype) for memory, x in zip(memories, arrays)],
         in_specs=[pl.BlockSpec(memory_space=pl.ANY)] * 4,
-        out_specs=[pl.BlockSpec(memory_space=pltpu.VMEM)] * 3,
-        scratch_shapes=[
-            pltpu.SMEM(frag_index.shape, jnp.int32),
-            pltpu.VMEM((frags, width), jnp.float32),
-            pltpu.SemaphoreType.DMA((4,)),
-        ],
+        out_specs=[pl.BlockSpec(memory_space=memory) for memory in memories],
+        scratch_shapes=[pltpu.SemaphoreType.DMA((4,))],
         name="begin",
-    )(frag_index, inner_params, outer_params, outer_momentum)
+    )(*arrays)
+
+
+def fold(columns, fragment, folded):
+    sublane = lax.broadcasted_iota(jnp.int32, (SUBLANES, LANES), 0)
+    turns = [(i + SUBLANES - fragment) % SUBLANES for i in range(SUBLANES)]
+    for top in range(0, folded.shape[0], SUBLANES):
+        tile = jnp.zeros((SUBLANES, LANES), jnp.float32)
+        for i in range(SUBLANES):
+            turned = pltpu.roll(columns(pl.ds((top + i) * LANES, LANES)), turns[i], 0)
+            tile = jnp.where(sublane == i, turned, tile)
+        folded[pl.ds(top, SUBLANES), :] = tile
+
+
+def drift_kernel(index, outer, inner, other, drift):
+    def both(at):
+        return (outer[:, at] - inner[0, :, at]) + (outer[:, at] - other[:, at])
+
+    fold(both, index[0], drift)
+
+
+def rows_kernel(index, outer, moment, outer_row, moment_row, chosen):
+    fold(lambda at: outer[:, at], index[0], outer_row)
+    fold(lambda at: moment[:, at], index[0], moment_row)
+    sublane = lax.broadcasted_iota(jnp.int32, chosen.shape, 0)
+    chosen[...] = (sublane == index[0]).astype(jnp.int32)
+
+
+def in_fast_memory(kernel, index, tables, shapes):
+    memory = pltpu.VMEM
+    return pl.pallas_call(
+        kernel,
+        out_shape=[memory(shape, dtype) for shape, dtype in shapes],
+        in_specs=[pl.BlockSpec(memory_space=pltpu.SMEM)]
+        + [pl.BlockSpec(memory_space=memory)] * len(tables),
+        out_specs=[pl.BlockSpec(memory_space=memory)] * len(shapes),
+        name=kernel.__name__,
+    )(index, *(pltpu.with_memory_space_constraint(table, memory) for table in tables))
 
 
 def swap(block, replica_bits, fsdp_bits):
@@ -120,25 +135,17 @@
     outer_params,
     outer_momentum,
 ):
-    fragment = frag_index[0]
     replicas = lax.axis_size("replica")
     frags, width = outer_params.shape
-    chosen = (jnp.arange(frags) == fragment)[:, None]
-
-    def row_of(table):
-        row = lax.dynamic_index_in_dim(table, fragment, 0, keepdims=False)
-        return row.reshape(width // LANES, LANES)
-
-    def put_row(row, table):
-        return jnp.where(chosen, row.reshape(1, width), table)
-
-    drift, outer_params, outer_momentum = begin(
+    other_inner = swap(inner_params[0], 1, 0)
+    index, inner_params, outer_params, outer_momentum = begin(
         frag_index, inner_params, outer_params, outer_momentum
     )
-    summed = drift + swap(drift, 1, 0)
-    inner_params, grads, adam_first, adam_second = after(
-        (inner_params, grads, adam_first, adam_second), summed
-    )
+    row = ((width // LANES, LANES), jnp.float32)
+    (summed,) = in_fast_memory(
+        drift_kernel, index, (outer_params, inner_params, other_inner), (row,)
+    )
+    (inner_params,) = after((inner_params,), summed)
     bit = 2
     while bit < replicas:
         summed = summed + swap(summed, bit | 1, 0)
@@ -154,7 +161,15 @@
         first_moment / first_fix
     ) / (jnp.sqrt(second_moment / second_fix) + adam_eps)
 
-    outer_row, moment_row = row_of(outer_params), row_of(outer_momentum)
+    outer_params, outer_momentum = after((outer_params, outer_momentum), stepped)
+    outer_row, moment_row, chosen = in_fast_memory(
+        rows_kernel, index, (outer_params, outer_momentum), (row, row, ((frags, LANES), jnp.int32))
+    )
+    chosen = chosen[:, :1] != 0
+
+    def put_row(row, table):
+        return jnp.where(chosen, row.reshape(1, width), table)
+
     new_outer_row, new_moment_row = nesterov(outer_row, moment_row, summed / replicas)
     refreshed_shard = new_outer_row.astype(jnp.bfloat16)
     held = gather_upper(refreshed_shard)

time: 19.1 us -> 18.5 us (0.969)
  waiting for transfers between devices: 4.04 us -> 3.49 us
    ppermute x6, waiting for transfers between devices: 4.04 us -> 3.49 us  [swap(): return lax.ppermute(block, AXES, pairs)]
    pallas_call x1 -> x3, Pallas kernels: 1.21 us -> 1.25 us  [the longest x1 1.16 us: begin(): pl.pallas_call(begin_kernel, out_shape=[memory(x.shape, x.dtype) for memo...]
  transfers between devices with their start and end apart: 6 -> 6, of which waited for: 6 -> 6; matrix products, arithmetic and copies ran while one was open for 15% -> 15% of each run, Pallas kernels for 0% -> 7%
where the time goes in v3:
time: 18.5 us; the launch traced here: 18.4 us
  starting transfers between devices  9.37 us (51%)
  waiting for transfers between devices  3.49 us (19%)
  other arithmetic  2.91 us (16%)
  Pallas kernels  1.25 us (7%)
  between operations  0.69 us (4%)
  local copies, waits for them, and re-layouts  0.68 us (4%)
    ppermute x6, starting transfers between devices, swap(): return lax.ppermute(block, AXES, pairs)  9.37 us
    ppermute x6, waiting for transfers between devices, swap(): return lax.ppermute(block, AXES, pairs)  3.49 us
    pallas_call x1, Pallas kernels, begin(): pl.pallas_call(begin_kernel, out_shape=[memory(x.shape, x.dtype) for memo...  1.16 us
    sub x1, other arithmetic, on_device(): inner_params * (1.0 - inner_rate * decay_rate)  1.01 us
    select_n x1, other arithmetic, put_row(): return jnp.where(chosen, row.reshape(1, width), table)  0.91 us
    select_n x1, other arithmetic, on_device(): new_inner = jnp.where(chosen[None], blended, stepped)  0.79 us
    another operation x1, local copies, waits for them, and re-layouts, gather_lower(): return jnp.stack(lower + upper, axis=1)  0.66 us
  transfers between devices with their start and end apart: 6, of which 6 were waited for; matrix products, arithmetic and copies ran while one was open for 15% of the time, Pallas kernels for 7%

profile of v3, /device:TPU:0, one launch (start us, length us, event | category | flops | bytes accessed | tf_op | source)
XLA Modules:
  0.0 18.4 jit_solution(7576399600935738277)
XLA Ops:
  0.6 0.5 %collective-permute-start = (f32[8,8192]{1,0:T(8,128)}, f32[8,8192]{1,0:T(8,128)S(1)}, u32[]{:S(2)}, u32[]{:S(2)}) collective-permute-start(f32[8,8192]{1,0:T(8,128)} %bitcast.32), channel_id=1, source_target_pairs={{0,8},{1,9},{2,10},{3,11},{4,12},{5,13},{6,14},{7,15},{8,0},{9,1},... | collective-permute-start | bytes 786440 | tf_op jit(solution)/shard_map/ppermute | solution.py:96
  1.2 0.0 copy-start.3
  1.2 1.2 %begin.1 = (s32[8]{0:T(128)S(4)}, f32[1,8,8192]{2,1,0:T(8,128)S(1)}, f32[8,8192]{1,0:T(8,128)S(1)}, f32[8,8192]{1,0:T(8,128)S(1)}) custom-call(s32[8]{0:T(128)} %refs_0_.1, f32[1,8,8192]{2,1,0:T(8,128)} %refs_1_.1, f32[8,8192]{1,0:T(8,128)} %refs_2_.1, f32[8,8192]{1,0:T(8,128)} %refs_3_.1), custom_call_target="tpu_custom_call" | custom-call | tf_op jit(solution)/shard_map/begin/pallas_call | solution.py:42
  2.3 0.0 copy-done.3
  2.3 0.2 collective-permute-done.other
  2.5 0.0 copy-start
  2.5 0.0 copy-start.1
  2.5 0.0 copy-start.2
  2.5 0.1 drift_kernel.1
  2.6 2.7 %collective-permute-start.1 = (f32[64,128]{1,0:T(8,128)S(1)}, f32[64,128]{1,0:T(8,128)S(1)}, u32[]{:S(2)}, u32[]{:S(2)}) collective-permute-start(f32[64,128]{1,0:T(8,128)S(1)} %drift_kernel.1), channel_id=1, source_target_pairs={{0,24},{1,25},{2,26},{3,27},{4,28},{5,29},{6,30},{7,31},{8,16},{9,... | collective-permute-start | bytes 98312 | tf_op jit(solution)/shard_map/ppermute | solution.py:96
  5.3 0.0 copy-done
  5.3 0.0 copy-done.1
  5.3 0.0 copy-done.2
  5.3 1.0 %divide_subtract_fusion = (f32[1,8,8192]{2,1,0:T(8,128)S(1)}, f32[1,8,8192]{2,1,0:T(8,128)}, f32[1,8,8192]{2,1,0:T(8,128)}) fusion(f32[1,8,8192]{2,1,0:T(8,128)S(1)} %get-tuple-element.22.inner, f32[8]{0:T(128)S(1)} %get-tuple-element.45, f32[8]{0:T(128)S(1)} %get-tuple-element.44, bf16[1,8,8192]{2,1,0:T(8,128)(2,1)S(1)} %copy-done.2, ...), kind=kLoop, calls=%fused_computation.5 | loop fusion | flops 983040 | bytes 1704000 | tf_op jit(solution)/shard_map/sub | solution.py:160
  6.3 0.1 fusion.3
  6.4 0.4 %collective-permute-done.1 = f32[64,128]{1,0:T(8,128)S(1)} collective-permute-done((f32[64,128]{1,0:T(8,128)S(1)}, f32[64,128]{1,0:T(8,128)S(1)}, u32[]{:S(2)}, u32[]{:S(2)}) %collective-permute-start.1) | collective-permute-done | bytes 32800 | tf_op jit(solution)/shard_map/ppermute | solution.py:96
  6.9 2.9 %collective-permute-start.2 = (bf16[1,64,128]{2,1,0:T(8,128)(2,1)S(1)}, bf16[1,64,128]{2,1,0:T(8,128)(2,1)S(1)}, u32[]{:S(2)}, u32[]{:S(2)}) collective-permute-start(bf16[1,64,128]{2,1,0:T(8,128)(2,1)S(1)} %bitcast.33), channel_id=1, source_target_pairs={{0,12},{1,13},{2,14},{3,15},{4,8},{5,9},{6,10},{7,11},{8,4},{9,5},... | collective-permute-start | bytes 49160 | tf_op jit(solution)/shard_map/ppermute | solution.py:96
  9.8 0.9 %broadcast_select_fusion = (f32[8,8192]{1,0:T(8,128)}, f32[8,8192]{1,0:T(8,128)}) fusion(f32[8,8192]{1,0:T(8,128)S(1)} %get-tuple-element.24.moment, f32[8192]{0:T(1024)S(1)} %get-tuple-element.39, pred[8]{0:T(512)(128)(4,1)S(1)} %fusion.3, f32[8,8192]{1,0:T(8,128)S(1)} %get-tuple-element.23.outer, f32[8192]{0:T(1024)S(1)} %bitcast.35), kind=kLoop, calls=%fused_computation.7 | loop fusion | flops 131072 | bytes 1114120 | tf_op jit(solution)/shard_map/jit(_where)/select_n | solution.py:171
  10.7 0.5 %collective-permute-done.2 = bf16[1,64,128]{2,1,0:T(8,128)(2,1)S(1)} collective-permute-done((bf16[1,64,128]{2,1,0:T(8,128)(2,1)S(1)}, bf16[1,64,128]{2,1,0:T(8,128)(2,1)S(1)}, u32[]{:S(2)}, u32[]{:S(2)}) %collective-permute-start.2) | collective-permute-done | bytes 16416 | tf_op jit(solution)/shard_map/ppermute | solution.py:96
  11.3 2.6 %collective-permute-start.4 = (bf16[2,64,128]{2,1,0:T(8,128)(2,1)S(1)}, bf16[2,64,128]{2,1,0:T(8,128)(2,1)S(1)}, u32[]{:S(2)}, u32[]{:S(2)}) collective-permute-start(bf16[2,64,128]{2,1,0:T(8,128)(2,1)S(1)} %maximum_bitcast_fusion), channel_id=1, source_target_pairs={{0,11},{1,10},{2,9},{3,8},{4,15},{5,14},{6,13},{7,12},{8,3},{9,2},... | collective-permute-start | bytes 98312 | tf_op jit(solution)/shard_map/ppermute | solution.py:96
  13.9 0.4 %collective-permute-start.5 = (bf16[2,64,128]{2,1,0:T(8,128)(2,1)S(1)}, bf16[2,64,128]{2,1,0:T(8,128)(2,1)S(1)}, u32[]{:S(2)}, u32[]{:S(2)}) collective-permute-start(bf16[2,64,128]{2,1,0:T(8,128)(2,1)S(1)} %maximum_bitcast_fusion), channel_id=1, source_target_pairs={{0,10},{1,11},{2,8},{3,9},{4,14},{5,15},{6,12},{7,13},{8,2},{9,3},... | collective-permute-start | bytes 98312 | tf_op jit(solution)/shard_map/ppermute | solution.py:96
  14.3 0.2 %collective-permute-start.3 = (bf16[2,64,128]{2,1,0:T(8,128)(2,1)S(1)}, bf16[2,64,128]{2,1,0:T(8,128)(2,1)S(1)}, u32[]{:S(2)}, u32[]{:S(2)}) collective-permute-start(bf16[2,64,128]{2,1,0:T(8,128)(2,1)S(1)} %maximum_bitcast_fusion), channel_id=1, source_target_pairs={{0,9},{1,8},{2,11},{3,10},{4,13},{5,12},{6,15},{7,14},{8,1},{9,0},... | collective-permute-start | bytes 98312 | tf_op jit(solution)/shard_map/ppermute | solution.py:96
  14.5 0.8 %add_select_fusion = f32[1,8,8192]{2,1,0:T(8,128)} fusion(f32[1,8,8192]{2,1,0:T(8,128)S(1)} %get-tuple-element.28, f32[8192]{0:T(1024)S(1)} %multiply_bitcast_fusion, pred[8]{0:T(512)(128)(4,1)S(1)} %fusion.3), kind=kLoop, calls=%fused_computation.4 | loop fusion | flops 196608 | bytes 557064 | tf_op jit(solution)/shard_map/jit(_where)/select_n | solution.py:182
  15.3 0.4 %collective-permute-done.4 = bf16[2,64,128]{2,1,0:T(8,128)(2,1)S(1)} collective-permute-done((bf16[2,64,128]{2,1,0:T(8,128)(2,1)S(1)}, bf16[2,64,128]{2,1,0:T(8,128)(2,1)S(1)}, u32[]{:S(2)}, u32[]{:S(2)}) %collective-permute-start.4) | collective-permute-done | bytes 32800 | tf_op jit(solution)/shard_map/ppermute | solution.py:96
  15.7 1.6 %collective-permute-done.5 = bf16[2,64,128]{2,1,0:T(8,128)(2,1)S(1)} collective-permute-done((bf16[2,64,128]{2,1,0:T(8,128)(2,1)S(1)}, bf16[2,64,128]{2,1,0:T(8,128)(2,1)S(1)}, u32[]{:S(2)}, u32[]{:S(2)}) %collective-permute-start.5) | collective-permute-done | bytes 32800 | tf_op jit(solution)/shard_map/ppermute | solution.py:96
  17.3 0.4 %collective-permute-done.3 = bf16[2,64,128]{2,1,0:T(8,128)(2,1)S(1)} collective-permute-done((bf16[2,64,128]{2,1,0:T(8,128)(2,1)S(1)}, bf16[2,64,128]{2,1,0:T(8,128)(2,1)S(1)}, u32[]{:S(2)}, u32[]{:S(2)}) %collective-permute-start.3) | collective-permute-done | bytes 32800 | tf_op jit(solution)/shard_map/ppermute | solution.py:96
  17.7 0.7 %copy.14 = bf16[2,4,64,128]{3,2,1,0:T(8,128)(2,1)} copy(bf16[2,4,64,128]{3,2,0,1:T(8,128)(2,1)S(1)} %pad_maximum_fusion) | data formatting | bytes 262144 | tf_op jit(solution)/shard_map/stack | solution.py:125
  (8 shorter events, 0.1 us)
Async XLA Ops:
  0.6 1.9 %collective-permute-start = (f32[8,8192]{1,0:T(8,128)}, f32[8,8192]{1,0:T(8,128)S(1)}, u32[]{:S(2)}, u32[]{:S(2)}) collective-permute-start(f32[8,8192]{1,0:T(8,128)} %bitcast.32), channel_id=1, source_target_pairs={{0,8},{1,9},{2,10},{3,11},{4,12},{5,13},{6,14},{7,15},{8,0},{9,1},... | collective-permute-start | bytes 786440 | tf_op jit(solution)/shard_map/ppermute | solution.py:96
  1.2 1.2 %copy-start.3 = (s32[8]{0:T(128)S(1)}, s32[8]{0:T(128)}, u32[]{:S(2)}) copy-start(s32[8]{0:T(128)} %param.9) | copy-start | bytes 100
  2.5 2.7 %copy-start = (f32[1,8,8192]{2,1,0:T(8,128)S(1)}, f32[1,8,8192]{2,1,0:T(8,128)}, u32[]{:S(2)}) copy-start(f32[1,8,8192]{2,1,0:T(8,128)} %param.12) | copy-start | bytes 786436
  2.5 2.7 %copy-start.1 = (f32[1,8,8192]{2,1,0:T(8,128)S(1)}, f32[1,8,8192]{2,1,0:T(8,128)}, u32[]{:S(2)}) copy-start(f32[1,8,8192]{2,1,0:T(8,128)} %param.13) | copy-start | bytes 786436
  2.5 2.7 %copy-start.2 = (bf16[1,8,8192]{2,1,0:T(8,128)(2,1)S(1)}, bf16[1,8,8192]{2,1,0:T(8,128)(2,1)}, u32[]{:S(2)}) copy-start(bf16[1,8,8192]{2,1,0:T(8,128)(2,1)} %param.11) | copy-start | bytes 393220
  2.6 4.3 %collective-permute-start.1 = (f32[64,128]{1,0:T(8,128)S(1)}, f32[64,128]{1,0:T(8,128)S(1)}, u32[]{:S(2)}, u32[]{:S(2)}) collective-permute-start(f32[64,128]{1,0:T(8,128)S(1)} %drift_kernel.1), channel_id=1, source_target_pairs={{0,24},{1,25},{2,26},{3,27},{4,28},{5,29},{6,30},{7,31},{8,16},{9,... | collective-permute-start | bytes 98312 | tf_op jit(solution)/shard_map/ppermute | solution.py:96
  6.9 4.4 %collective-permute-start.2 = (bf16[1,64,128]{2,1,0:T(8,128)(2,1)S(1)}, bf16[1,64,128]{2,1,0:T(8,128)(2,1)S(1)}, u32[]{:S(2)}, u32[]{:S(2)}) collective-permute-start(bf16[1,64,128]{2,1,0:T(8,128)(2,1)S(1)} %bitcast.33), channel_id=1, source_target_pairs={{0,12},{1,13},{2,14},{3,15},{4,8},{5,9},{6,10},{7,11},{8,4},{9,5},... | collective-permute-start | bytes 49160 | tf_op jit(solution)/shard_map/ppermute | solution.py:96
  11.3 4.4 %collective-permute-start.4 = (bf16[2,64,128]{2,1,0:T(8,128)(2,1)S(1)}, bf16[2,64,128]{2,1,0:T(8,128)(2,1)S(1)}, u32[]{:S(2)}, u32[]{:S(2)}) collective-permute-start(bf16[2,64,128]{2,1,0:T(8,128)(2,1)S(1)} %maximum_bitcast_fusion), channel_id=1, source_target_pairs={{0,11},{1,10},{2,9},{3,8},{4,15},{5,14},{6,13},{7,12},{8,3},{9,2},... | collective-permute-start | bytes 98312 | tf_op jit(solution)/shard_map/ppermute | solution.py:96
  13.9 3.4 %collective-permute-start.5 = (bf16[2,64,128]{2,1,0:T(8,128)(2,1)S(1)}, bf16[2,64,128]{2,1,0:T(8,128)(2,1)S(1)}, u32[]{:S(2)}, u32[]{:S(2)}) collective-permute-start(bf16[2,64,128]{2,1,0:T(8,128)(2,1)S(1)} %maximum_bitcast_fusion), channel_id=1, source_target_pairs={{0,10},{1,11},{2,8},{3,9},{4,14},{5,15},{6,12},{7,13},{8,2},{9,3},... | collective-permute-start | bytes 98312 | tf_op jit(solution)/shard_map/ppermute | solution.py:96
  14.3 3.4 %collective-permute-start.3 = (bf16[2,64,128]{2,1,0:T(8,128)(2,1)S(1)}, bf16[2,64,128]{2,1,0:T(8,128)(2,1)S(1)}, u32[]{:S(2)}, u32[]{:S(2)}) collective-permute-start(bf16[2,64,128]{2,1,0:T(8,128)(2,1)S(1)} %maximum_bitcast_fusion), channel_id=1, source_target_pairs={{0,9},{1,8},{2,11},{3,10},{4,13},{5,12},{6,15},{7,14},{8,1},{9,0},... | collective-permute-start | bytes 98312 | tf_op jit(solution)/shard_map/ppermute | solution.py:96

commit v4 on v3

--- a/solution.py
+++ b/solution.py
@@ -17,12 +17,6 @@
 AXES = ("replica", "fsdp")
 LANES = 128
 SUBLANES = 8
-
-
-def nesterov(outer_row, moment_row, mean_drift):
-    new_moment_row = momentum_keep * moment_row + mean_drift
-    new_outer_row = outer_row - outer_rate * (mean_drift + momentum_keep * new_moment_row)
-    return (new_outer_row, new_moment_row)
 
 
 def begin_kernel(*refs):
@@ -60,16 +54,14 @@
         folded[pl.ds(top, SUBLANES), :] = tile
 
 
-def drift_kernel(index, outer, inner, other, drift):
-    def both(at):
+def rows_kernel(index, outer, inner, other, moment, drift, share, moment_row, chosen):
+    def drifts(at):
         return (outer[:, at] - inner[0, :, at]) + (outer[:, at] - other[:, at])
 
-    fold(both, index[0], drift)
-
-
-def rows_kernel(index, outer, moment, outer_row, moment_row, chosen):
-    fold(lambda at: outer[:, at], index[0], outer_row)
+    fold(drifts, index[0], drift)
     fold(lambda at: moment[:, at], index[0], moment_row)
+    fold(lambda at: outer[:, at], index[0], share)
+    share[...] = 0.5 * (share[...] - outer_rate * momentum_keep * momentum_keep * moment_row[...])
     sublane = lax.broadcasted_iota(jnp.int32, chosen.shape, 0)
     chosen[...] = (sublane == index[0]).astype(jnp.int32)
 
@@ -100,29 +92,30 @@
     return lax.optimization_barrier((tuple(arrays), earlier))[0]
 
 
-def gather_upper(block):
-    shard = lax.axis_index("fsdp")
-    held = block[None]
-    bit = lax.axis_size("fsdp") // 2
-    while bit > 2:
-        other = swap(held, 1, bit)
-        upper = (shard & bit) != 0
-        held = jnp.stack(
-            [jnp.where(upper, other, held), jnp.where(upper, held, other)], axis=1
-        ).reshape(-1, *block.shape)
-        bit //= 2
-    return held
-
-
-def gather_lower(held):
-    shard = lax.axis_index("fsdp")
-    first, second, both = (swap(held, 1, bits) for bits in (1, 2, 3))
-    even, odd, low = (shard & 1) == 0, (shard & 1) != 0, (shard & 2) == 0
-    near = (jnp.where(even, held, first), jnp.where(even, first, held))
-    far = (jnp.where(odd, both, second), jnp.where(odd, second, both))
-    lower = [jnp.where(low, n, f) for n, f in zip(near, far)]
-    upper = [jnp.where(low, f, n) for n, f in zip(near, far)]
-    return jnp.stack(lower + upper, axis=1)
+def bit_of(axis, bit):
+    return (lax.axis_index(axis) & bit) != 0
+
+
+def ring(near, far, replica_bit, fsdp_bits):
+    fsdp_a, fsdp_b = fsdp_bits
+    replicas, shards = lax.axis_size("replica"), lax.axis_size("fsdp")
+    pairs = []
+    for r in range(replicas):
+        for s in range(shards):
+            a = (r & replica_bit) != 0 or (s & fsdp_a) != 0
+            across = s ^ fsdp_a if (r & 1) == a else s ^ fsdp_a ^ fsdp_b
+            pairs.append((r * shards + s, (r ^ replica_bit ^ 1) * shards + across))
+    got = lax.ppermute(far, AXES, pairs)
+    across_b = swap(near, 1, fsdp_b)
+    other = swap(got, 1, 0)
+    got, other, across_b = lax.optimization_barrier((got, other, across_b))
+    a = bit_of("replica", replica_bit) | bit_of("fsdp", fsdp_a)
+    is_a = bit_of("replica", 1) == a
+    return jnp.where(is_a, got, other), across_b, jnp.where(is_a, other, got)
+
+
+def in_order(bit, own, other):
+    return jnp.where(bit, other, own), jnp.where(bit, own, other)
 
 
 def on_device(
@@ -142,15 +135,33 @@
         frag_index, inner_params, outer_params, outer_momentum
     )
     row = ((width // LANES, LANES), jnp.float32)
-    (summed,) = in_fast_memory(
-        drift_kernel, index, (outer_params, inner_params, other_inner), (row,)
-    )
-    (inner_params,) = after((inner_params,), summed)
+    drift, share, moment_row, chosen = in_fast_memory(
+        rows_kernel,
+        index,
+        (outer_params, inner_params, other_inner, outer_momentum),
+        (row, row, row, ((frags, LANES), jnp.int32)),
+    )
+    chosen = chosen[:, :1] != 0
+
+    def put_row(row, table):
+        return jnp.where(chosen, row.reshape(1, width), table)
+
+    half = replicas // 2
     bit = 2
-    while bit < replicas:
-        summed = summed + swap(summed, bit | 1, 0)
+    while bit < half:
+        drift = drift + swap(drift, bit | 1, 0)
         bit *= 2
 
+    def part(drift):
+        return share - (outer_rate * (1.0 + momentum_keep) / replicas) * drift
+
+    same_row = bit_of("replica", 1) == bit_of("replica", half)
+    far = jnp.where(same_row, drift, part(drift))
+    drift_across, near_across, far_across = ring(part(drift), far, half, (0, 2))
+
+    inner_params, outer_params, outer_momentum = after(
+        (inner_params, outer_params, outer_momentum), far
+    )
     step_count = inner_step.astype(jnp.float32)[None, :, None]
     grad_wide = grads.astype(jnp.float32)
     first_moment = beta_first * adam_first + (1.0 - beta_first) * grad_wide
@@ -161,22 +172,27 @@
         first_moment / first_fix
     ) / (jnp.sqrt(second_moment / second_fix) + adam_eps)
 
-    outer_params, outer_momentum = after((outer_params, outer_momentum), stepped)
-    outer_row, moment_row, chosen = in_fast_memory(
-        rows_kernel, index, (outer_params, outer_momentum), (row, row, ((frags, LANES), jnp.int32))
-    )
-    chosen = chosen[:, :1] != 0
-
-    def put_row(row, table):
-        return jnp.where(chosen, row.reshape(1, width), table)
-
-    new_outer_row, new_moment_row = nesterov(outer_row, moment_row, summed / replicas)
+    mean_drift = (drift + drift_across) / replicas
+    new_moment_row = momentum_keep * moment_row + mean_drift
+    new_outer_row = part(drift) + part(drift_across)
     refreshed_shard = new_outer_row.astype(jnp.bfloat16)
-    held = gather_upper(refreshed_shard)
+    next_shard = (near_across + far_across).astype(jnp.bfloat16)
+    held = jnp.stack(in_order(bit_of("fsdp", 2), refreshed_shard, next_shard))
+    bit = 8
+    while bit < lax.axis_size("fsdp"):
+        held = jnp.stack(in_order(bit_of("fsdp", bit), held, swap(held, 1, bit)))
+        bit *= 2
+    across_4, across_1, across_5 = ring(held, held, 0, (4, 1))
+    odd = bit_of("fsdp", 1)
+    own_4 = jnp.stack(in_order(odd, held, across_1), axis=-3)
+    other_4 = jnp.stack(in_order(odd, across_4, across_5), axis=-3)
+    refreshed = jnp.stack(in_order(bit_of("fsdp", 4), own_4, other_4), axis=-5).reshape(-1)
+
+    stepped, refreshed_shard, outer_params, outer_momentum = after(
+        (stepped, refreshed_shard, outer_params, outer_momentum), held
+    )
     new_outer = put_row(new_outer_row, outer_params)
     new_momentum = put_row(new_moment_row, outer_momentum)
-    refreshed = gather_lower(held).reshape(-1)
-    stepped, refreshed_shard = after((stepped, refreshed_shard), held)
     refreshed_row = refreshed_shard.astype(jnp.float32).reshape(1, 1, width)
     blended = mix_local * stepped + (1.0 - mix_local) * refreshed_row
     new_inner = jnp.where(chosen[None], blended, stepped)

time: 18.5 us -> 17.1 us (0.924)
  waiting for transfers between devices: 3.49 us -> 1 us
  starting transfers between devices: 9.37 us -> 10.3 us
    ppermute x0 -> x2, starting transfers between devices: none -> 5.81 us  [ring(): got = lax.ppermute(far, AXES, pairs)]
    ppermute x6 -> x5, starting transfers between devices: 9.37 us -> 4.5 us  [swap(): return lax.ppermute(block, AXES, pairs)]
    ppermute x6 -> x5, waiting for transfers between devices: 3.49 us -> 0.99 us  [swap(): return lax.ppermute(block, AXES, pairs)]
  transfers between devices with their start and end apart: 6 -> 7, of which waited for: 6 -> 4; matrix products, arithmetic and copies ran while one was open for 15% -> 17% of each run, Pallas kernels for 7% -> 7%
where the time goes in v4:
time: 17.1 us; the launch traced here: 16.9 us
  starting transfers between devices  10.3 us (60%)
  other arithmetic  2.95 us (17%)
  Pallas kernels  1.25 us (7%)
  waiting for transfers between devices  1 us (6%)
  between operations  0.73 us (4%)
  local copies, waits for them, and re-layouts  0.68 us (4%)
    ppermute x2, starting transfers between devices, ring(): got = lax.ppermute(far, AXES, pairs)  5.81 us
    ppermute x5, starting transfers between devices, swap(): return lax.ppermute(block, AXES, pairs)  4.5 us
    pallas_call x1, Pallas kernels, begin(): pl.pallas_call(begin_kernel, out_shape=[memory(x.shape, x.dtype) for memo...  1.16 us
    sub x1, other arithmetic, on_device(): inner_params * (1.0 - inner_rate * decay_rate)  1.01 us
    ppermute x5, waiting for transfers between devices, swap(): return lax.ppermute(block, AXES, pairs)  0.99 us
    select_n x1, other arithmetic, put_row(): return jnp.where(chosen, row.reshape(1, width), table)  0.92 us
    select_n x1, other arithmetic, on_device(): new_inner = jnp.where(chosen[None], blended, stepped)  0.79 us
    another operation x1, local copies, waits for them, and re-layouts, on_device(): jnp.stack(in_order(bit_of('fsdp', 4), own_4, other_4), axis=-5).reshape(-1)  0.66 us
  transfers between devices with their start and end apart: 7, of which 4 were waited for; matrix products, arithmetic and copies ran while one was open for 17% of the time, Pallas kernels for 7%

profile of v4, /device:TPU:0, one launch (start us, length us, event | category | flops | bytes accessed | tf_op | source)
XLA Modules:
  0.0 16.9 jit_solution(7469669202191432294)
XLA Ops:
  0.6 0.5 %collective-permute-start = (f32[8,8192]{1,0:T(8,128)}, f32[8,8192]{1,0:T(8,128)S(1)}, u32[]{:S(2)}, u32[]{:S(2)}) collective-permute-start(f32[8,8192]{1,0:T(8,128)} %bitcast.19), channel_id=1, source_target_pairs={{0,8},{1,9},{2,10},{3,11},{4,12},{5,13},{6,14},{7,15},{8,0},{9,1},... | collective-permute-start | bytes 786440 | tf_op jit(solution)/shard_map/ppermute | solution.py:88
  1.2 0.0 copy-start.3
  1.2 1.2 %begin.1 = (s32[8]{0:T(128)S(4)}, f32[1,8,8192]{2,1,0:T(8,128)S(1)}, f32[8,8192]{1,0:T(8,128)S(1)}, f32[8,8192]{1,0:T(8,128)S(1)}) custom-call(s32[8]{0:T(128)} %refs_0_.1, f32[1,8,8192]{2,1,0:T(8,128)} %refs_1_.1, f32[8,8192]{1,0:T(8,128)} %refs_2_.1, f32[8,8192]{1,0:T(8,128)} %refs_3_.1), custom_call_target="tpu_custom_call" | custom-call | tf_op jit(solution)/shard_map/begin/pallas_call | solution.py:36
  2.3 0.0 copy-done.3
  2.3 0.2 %collective-permute-done.other = f32[8,8192]{1,0:T(8,128)S(1)} collective-permute-done((f32[8,8192]{1,0:T(8,128)}, f32[8,8192]{1,0:T(8,128)S(1)}, u32[]{:S(2)}, u32[]{:S(2)}) %collective-permute-start) | collective-permute-done | bytes 262176 | tf_op jit(solution)/shard_map/ppermute | solution.py:88
  2.5 0.0 copy-start
  2.5 0.0 copy-start.1
  2.5 0.1 rows_kernel.1
  2.6 0.0 copy-start.2
  2.7 2.7 %collective-permute-start.1 = (f32[64,128]{1,0:T(8,128)S(1)}, f32[64,128]{1,0:T(8,128)S(1)}, u32[]{:S(2)}, u32[]{:S(2)}) collective-permute-start(f32[64,128]{1,0:T(8,128)S(1)} %get-tuple-element.62), channel_id=1, source_target_pairs={{0,24},{1,25},{2,26},{3,27},{4,28},{5,29},{6,30},{7,31},{8,18},{9,... | collective-permute-start | bytes 98312 | tf_op jit(solution)/shard_map/ppermute | solution.py:108
  5.3 1.4 %collective-permute-start.3 = (f32[64,128]{1,0:T(8,128)S(1)}, f32[64,128]{1,0:T(8,128)S(1)}, u32[]{:S(2)}, u32[]{:S(2)}) collective-permute-start(f32[64,128]{1,0:T(8,128)S(1)} %get-tuple-element.61), channel_id=1, source_target_pairs={{0,10},{1,11},{2,8},{3,9},{4,14},{5,15},{6,12},{7,13},{8,2},{9,3},... | collective-permute-start | bytes 98312 | tf_op jit(solution)/shard_map/ppermute | solution.py:88
  6.8 0.0 copy-done
  6.8 0.0 copy-done.1
  6.8 0.0 copy-done.2
  6.8 1.0 %divide_subtract_fusion = (f32[1,8,8192]{2,1,0:T(8,128)S(1)}, f32[1,8,8192]{2,1,0:T(8,128)}, f32[1,8,8192]{2,1,0:T(8,128)}) fusion(f32[1,8,8192]{2,1,0:T(8,128)S(1)} %get-tuple-element.34.inner, f32[8]{0:T(128)S(1)} %get-tuple-element.66, f32[8]{0:T(128)S(1)} %get-tuple-element.65, bf16[1,8,8192]{2,1,0:T(8,128)(2,1)S(1)} %copy-done.2, ...), kind=kLoop, calls=%fused_computation.5 | loop fusion | flops 983040 | bytes 1704000 | tf_op jit(solution)/shard_map/sub | solution.py:171
  7.8 0.0 collective-permute-done.1
  7.8 0.5 %collective-permute-start.2 = (f32[64,128]{1,0:T(8,128)S(1)}, f32[64,128]{1,0:T(8,128)S(1)}, u32[]{:S(2)}, u32[]{:S(2)}) collective-permute-start(f32[64,128]{1,0:T(8,128)S(1)} %collective-permute-done.1), channel_id=1, source_target_pairs={{0,8},{1,9},{2,10},{3,11},{4,12},{5,13},{6,14},{7,15},{8,0},{9,1},... | collective-permute-start | bytes 98312 | tf_op jit(solution)/shard_map/ppermute | solution.py:88
  8.3 0.1 fusion.2
  8.4 0.3 %collective-permute-done.3 = f32[64,128]{1,0:T(8,128)S(1)} collective-permute-done((f32[64,128]{1,0:T(8,128)S(1)}, f32[64,128]{1,0:T(8,128)S(1)}, u32[]{:S(2)}, u32[]{:S(2)}) %collective-permute-start.3) | collective-permute-done | bytes 32800 | tf_op jit(solution)/shard_map/ppermute | solution.py:88
  8.7 0.5 %collective-permute-done.2 = f32[64,128]{1,0:T(8,128)S(1)} collective-permute-done((f32[64,128]{1,0:T(8,128)S(1)}, f32[64,128]{1,0:T(8,128)S(1)}, u32[]{:S(2)}, u32[]{:S(2)}) %collective-permute-start.2) | collective-permute-done | bytes 32800 | tf_op jit(solution)/shard_map/ppermute | solution.py:88
  9.2 3.1 %collective-permute-start.4 = (bf16[2,64,128]{2,1,0:T(8,128)(2,1)S(1)}, bf16[2,64,128]{2,1,0:T(8,128)(2,1)S(1)}, u32[]{:S(2)}, u32[]{:S(2)}) collective-permute-start(bf16[2,64,128]{2,1,0:T(8,128)(2,1)S(1)} %pad_maximum_fusion.3), channel_id=1, source_target_pairs={{0,12},{1,13},{2,14},{3,15},{4,9},{5,8},{6,11},{7,10},{8,5},{9,4},... | collective-permute-start | bytes 98312 | tf_op jit(solution)/shard_map/ppermute | solution.py:108
  12.4 0.8 %collective-permute-start.6 = (bf16[2,64,128]{2,1,0:T(8,128)(2,1)S(1)}, bf16[2,64,128]{2,1,0:T(8,128)(2,1)S(1)}, u32[]{:S(2)}, u32[]{:S(2)}) collective-permute-start(bf16[2,64,128]{2,1,0:T(8,128)(2,1)S(1)} %pad_maximum_fusion.3), channel_id=1, source_target_pairs={{0,9},{1,8},{2,11},{3,10},{4,13},{5,12},{6,15},{7,14},{8,1},{9,0},... | collective-permute-start | bytes 98312 | tf_op jit(solution)/shard_map/ppermute | solution.py:88
  13.2 0.9 %broadcast_select_fusion = (f32[8,8192]{1,0:T(8,128)}, f32[8,8192]{1,0:T(8,128)}) fusion(f32[8,8192]{1,0:T(8,128)S(1)} %get-tuple-element.44.moment, f32[8192]{0:T(1024)S(1)} %add_bitcast_fusion, pred[8]{0:T(512)(128)(4,1)S(1)} %fusion.2, f32[8,8192]{1,0:T(8,128)S(1)} %get-tuple-element.42.outer, f32[8192]{0:T(1024)S(1)} %bitcast.20), kind=kLoop, calls=%fused_computation.7 | loop fusion | flops 131072 | bytes 1114120 | tf_op jit(solution)/shard_map/jit(_where)/select_n | solution.py:147
  14.2 0.0 collective-permute-done.4
  14.2 1.2 %collective-permute-start.5 = (bf16[2,64,128]{2,1,0:T(8,128)(2,1)S(1)}, bf16[2,64,128]{2,1,0:T(8,128)(2,1)S(1)}, u32[]{:S(2)}, u32[]{:S(2)}) collective-permute-start(bf16[2,64,128]{2,1,0:T(8,128)(2,1)S(1)} %collective-permute-done.4), channel_id=1, source_target_pairs={{0,8},{1,9},{2,10},{3,11},{4,12},{5,13},{6,14},{7,15},{8,0},{9,1},... | collective-permute-start | bytes 98312 | tf_op jit(solution)/shard_map/ppermute | solution.py:88
  15.3 0.8 %add_select_fusion = f32[1,8,8192]{2,1,0:T(8,128)} fusion(f32[1,8,8192]{2,1,0:T(8,128)S(1)} %get-tuple-element.40, f32[8192]{0:T(1024)S(1)} %multiply_bitcast_fusion, pred[8]{0:T(512)(128)(4,1)S(1)} %fusion.2), kind=kLoop, calls=%fused_computation.4 | loop fusion | flops 196608 | bytes 557064 | tf_op jit(solution)/shard_map/jit(_where)/select_n | solution.py:198
  16.1 0.0 collective-permute-done.6
  16.1 0.1 collective-permute-done.5
  16.2 0.7 %copy.14 = bf16[2,2,2,64,128]{4,3,2,1,0:T(8,128)(2,1)} copy(bf16[2,2,2,64,128]{4,3,1,2,0:T(8,128)(2,1)S(1)} %pad_maximum_fusion) | data formatting | bytes 262144 | tf_op jit(solution)/shard_map/stack | solution.py:189
  (10 shorter events, 0.1 us)
Async XLA Ops:
  0.6 1.9 %collective-permute-start = (f32[8,8192]{1,0:T(8,128)}, f32[8,8192]{1,0:T(8,128)S(1)}, u32[]{:S(2)}, u32[]{:S(2)}) collective-permute-start(f32[8,8192]{1,0:T(8,128)} %bitcast.19), channel_id=1, source_target_pairs={{0,8},{1,9},{2,10},{3,11},{4,12},{5,13},{6,14},{7,15},{8,0},{9,1},... | collective-permute-start | bytes 786440 | tf_op jit(solution)/shard_map/ppermute | solution.py:88
  1.2 1.2 %copy-start.3 = (s32[8]{0:T(128)S(1)}, s32[8]{0:T(128)}, u32[]{:S(2)}) copy-start(s32[8]{0:T(128)} %param.9) | copy-start | bytes 100
  2.5 4.2 %copy-start = (f32[1,8,8192]{2,1,0:T(8,128)S(1)}, f32[1,8,8192]{2,1,0:T(8,128)}, u32[]{:S(2)}) copy-start(f32[1,8,8192]{2,1,0:T(8,128)} %param.12) | copy-start | bytes 786436
  2.5 4.2 %copy-start.1 = (f32[1,8,8192]{2,1,0:T(8,128)S(1)}, f32[1,8,8192]{2,1,0:T(8,128)}, u32[]{:S(2)}) copy-start(f32[1,8,8192]{2,1,0:T(8,128)} %param.13) | copy-start | bytes 786436
  2.6 4.1 %copy-start.2 = (bf16[1,8,8192]{2,1,0:T(8,128)(2,1)S(1)}, bf16[1,8,8192]{2,1,0:T(8,128)(2,1)}, u32[]{:S(2)}) copy-start(bf16[1,8,8192]{2,1,0:T(8,128)(2,1)} %param.11) | copy-start | bytes 393220
  2.7 5.1 %collective-permute-start.1 = (f32[64,128]{1,0:T(8,128)S(1)}, f32[64,128]{1,0:T(8,128)S(1)}, u32[]{:S(2)}, u32[]{:S(2)}) collective-permute-start(f32[64,128]{1,0:T(8,128)S(1)} %get-tuple-element.62), channel_id=1, source_target_pairs={{0,24},{1,25},{2,26},{3,27},{4,28},{5,29},{6,30},{7,31},{8,18},{9,... | collective-permute-start | bytes 98312 | tf_op jit(solution)/shard_map/ppermute | solution.py:108
  5.3 3.4 %collective-permute-start.3 = (f32[64,128]{1,0:T(8,128)S(1)}, f32[64,128]{1,0:T(8,128)S(1)}, u32[]{:S(2)}, u32[]{:S(2)}) collective-permute-start(f32[64,128]{1,0:T(8,128)S(1)} %get-tuple-element.61), channel_id=1, source_target_pairs={{0,10},{1,11},{2,8},{3,9},{4,14},{5,15},{6,12},{7,13},{8,2},{9,3},... | collective-permute-start | bytes 98312 | tf_op jit(solution)/shard_map/ppermute | solution.py:88
  7.8 1.4 %collective-permute-start.2 = (f32[64,128]{1,0:T(8,128)S(1)}, f32[64,128]{1,0:T(8,128)S(1)}, u32[]{:S(2)}, u32[]{:S(2)}) collective-permute-start(f32[64,128]{1,0:T(8,128)S(1)} %collective-permute-done.1), channel_id=1, source_target_pairs={{0,8},{1,9},{2,10},{3,11},{4,12},{5,13},{6,14},{7,15},{8,0},{9,1},... | collective-permute-start | bytes 98312 | tf_op jit(solution)/shard_map/ppermute | solution.py:88
  9.2 4.9 %collective-permute-start.4 = (bf16[2,64,128]{2,1,0:T(8,128)(2,1)S(1)}, bf16[2,64,128]{2,1,0:T(8,128)(2,1)S(1)}, u32[]{:S(2)}, u32[]{:S(2)}) collective-permute-start(bf16[2,64,128]{2,1,0:T(8,128)(2,1)S(1)} %pad_maximum_fusion.3), channel_id=1, source_target_pairs={{0,12},{1,13},{2,14},{3,15},{4,9},{5,8},{6,11},{7,10},{8,5},{9,4},... | collective-permute-start | bytes 98312 | tf_op jit(solution)/shard_map/ppermute | solution.py:108
  12.4 3.7 %collective-permute-start.6 = (bf16[2,64,128]{2,1,0:T(8,128)(2,1)S(1)}, bf16[2,64,128]{2,1,0:T(8,128)(2,1)S(1)}, u32[]{:S(2)}, u32[]{:S(2)}) collective-permute-start(bf16[2,64,128]{2,1,0:T(8,128)(2,1)S(1)} %pad_maximum_fusion.3), channel_id=1, source_target_pairs={{0,9},{1,8},{2,11},{3,10},{4,13},{5,12},{6,15},{7,14},{8,1},{9,0},... | collective-permute-start | bytes 98312 | tf_op jit(solution)/shard_map/ppermute | solution.py:88
  14.2 2.0 %collective-permute-start.5 = (bf16[2,64,128]{2,1,0:T(8,128)(2,1)S(1)}, bf16[2,64,128]{2,1,0:T(8,128)(2,1)S(1)}, u32[]{:S(2)}, u32[]{:S(2)}) collective-permute-start(bf16[2,64,128]{2,1,0:T(8,128)(2,1)S(1)} %collective-permute-done.4), channel_id=1, source_target_pairs={{0,8},{1,9},{2,10},{3,11},{4,12},{5,13},{6,14},{7,15},{8,0},{9,1},... | collective-permute-start | bytes 98312 | tf_op jit(solution)/shard_map/ppermute | solution.py:88

commit v5 on v4

--- a/solution.py
+++ b/solution.py
@@ -111,11 +111,48 @@
     got, other, across_b = lax.optimization_barrier((got, other, across_b))
     a = bit_of("replica", replica_bit) | bit_of("fsdp", fsdp_a)
     is_a = bit_of("replica", 1) == a
-    return jnp.where(is_a, got, other), across_b, jnp.where(is_a, other, got)
+    return got, other, across_b, is_a
 
 
 def in_order(bit, own, other):
     return jnp.where(bit, other, own), jnp.where(bit, own, other)
+
+
+def order_kernel(own, across_1, got, other, refreshed, sems):
+    core = lax.axis_index("replica") % 2
+    four, one = (lax.axis_index("fsdp") // 4) % 2, lax.axis_index("fsdp") % 2
+    straight = (core + four + 1) % 2
+    far = ((one + 1 + straight) % 2, (one + straight) % 2)
+    blocks, rows = own.shape[0], own.shape[1]
+    copies = []
+    for source, at_4, at_1 in (
+        (own, four, one),
+        (across_1, four, 1 - one),
+        (got, 1 - four, far[0]),
+        (other, 1 - four, far[1]),
+    ):
+        for i in range(blocks):
+            place = ((i // 2 * 2 + at_4) * 2 + i % 2) * 2 + at_1
+            target = refreshed.at[pl.ds(pl.multiple_of(place * rows, rows), rows), :]
+            copies.append(pltpu.make_async_copy(source.at[i], target, sems.at[len(copies)]))
+    for copy in copies:
+        copy.start()
+    for copy in copies:
+        copy.wait()
+
+
+def put_in_order(*sources):
+    rows, lanes = sources[0].shape[-2:]
+    sources = [x.reshape(-1, rows, lanes) for x in sources]
+    count = 4 * sources[0].shape[0]
+    return pl.pallas_call(
+        order_kernel,
+        out_shape=jax.ShapeDtypeStruct((count * rows, lanes), sources[0].dtype),
+        in_specs=[pl.BlockSpec(memory_space=pltpu.VMEM)] * 4,
+        out_specs=pl.BlockSpec(memory_space=pltpu.HBM),
+        scratch_shapes=[pltpu.SemaphoreType.DMA((count,))],
+        name="order",
+    )(*(pltpu.with_memory_space_constraint(x, pltpu.VMEM) for x in sources)).reshape(-1)
 
 
 def on_device(
@@ -157,7 +194,8 @@
 
     same_row = bit_of("replica", 1) == bit_of("replica", half)
     far = jnp.where(same_row, drift, part(drift))
-    drift_across, near_across, far_across = ring(part(drift), far, half, (0, 2))
+    got, other, near_across, is_a = ring(part(drift), far, half, (0, 2))
+    drift_across, far_across = jnp.where(is_a, got, other), jnp.where(is_a, other, got)
 
     inner_params, outer_params, outer_momentum = after(
         (inner_params, outer_params, outer_momentum), far
@@ -182,11 +220,8 @@
     while bit < lax.axis_size("fsdp"):
         held = jnp.stack(in_order(bit_of("fsdp", bit), held, swap(held, 1, bit)))
         bit *= 2
-    across_4, across_1, across_5 = ring(held, held, 0, (4, 1))
-    odd = bit_of("fsdp", 1)
-    own_4 = jnp.stack(in_order(odd, held, across_1), axis=-3)
-    other_4 = jnp.stack(in_order(odd, across_4, across_5), axis=-3)
-    refreshed = jnp.stack(in_order(bit_of("fsdp", 4), own_4, other_4), axis=-5).reshape(-1)
+    got, other, across_1, _ = ring(held, held, 0, (4, 1))
+    refreshed = put_in_order(held, across_1, got, other)
 
     stepped, refreshed_shard, outer_params, outer_momentum = after(
         (stepped, refreshed_shard, outer_params, outer_momentum), held

time: 17.1 us -> 17 us (level)
  Pallas kernels: 1.25 us -> 1.96 us
  local copies, waits for them, and re-layouts: 0.68 us -> 0.02 us
    pallas_call x0 -> x1, Pallas kernels: none -> 0.71 us  [put_in_order(): pl.pallas_call(order_kernel, out_shape=jax.ShapeDtypeStruct((count * rows...]
    another operation x1 -> x0, local copies, waits for them, and re-layouts: 0.66 us -> none  [on_device(): jnp.stack(in_order(bit_of('fsdp', 4), own_4, other_4), axis=-5).reshape(-1)]
where the time goes in v5:
time: 17 us; the launch traced here: 16.9 us
  starting transfers between devices  10.3 us (61%)
  other arithmetic  2.89 us (17%)
  Pallas kernels  1.96 us (12%)
  waiting for transfers between devices  1 us (6%)
  between operations  0.71 us (4%)
    ppermute x2, starting transfers between devices, ring(): got = lax.ppermute(far, AXES, pairs)  5.81 us
    ppermute x5, starting transfers between devices, swap(): return lax.ppermute(block, AXES, pairs)  4.5 us
    pallas_call x1, Pallas kernels, begin(): pl.pallas_call(begin_kernel, out_shape=[memory(x.shape, x.dtype) for memo...  1.16 us
    sub x1, other arithmetic, on_device(): inner_params * (1.0 - inner_rate * decay_rate)  1.01 us
    ppermute x5, waiting for transfers between devices, swap(): return lax.ppermute(block, AXES, pairs)  0.99 us
    select_n x1, other arithmetic, put_row(): return jnp.where(chosen, row.reshape(1, width), table)  0.91 us
    select_n x1, other arithmetic, on_device(): new_inner = jnp.where(chosen[None], blended, stepped)  0.79 us
    pallas_call x1, Pallas kernels, put_in_order(): pl.pallas_call(order_kernel, out_shape=jax.ShapeDtypeStruct((count * rows...  0.71 us
  transfers between devices with their start and end apart: 7, of which 4 were waited for; matrix products, arithmetic and copies ran while one was open for 17% of the time, Pallas kernels for 7%

profile of v5, /device:TPU:0, one launch (start us, length us, event | category | flops | bytes accessed | tf_op | source)
XLA Modules:
  0.0 16.9 jit_solution(8444192763152346054)
XLA Ops:
  0.6 0.5 %collective-permute-start = (f32[8,8192]{1,0:T(8,128)}, f32[8,8192]{1,0:T(8,128)S(1)}, u32[]{:S(2)}, u32[]{:S(2)}) collective-permute-start(f32[8,8192]{1,0:T(8,128)} %bitcast.11), channel_id=1, source_target_pairs={{0,8},{1,9},{2,10},{3,11},{4,12},{5,13},{6,14},{7,15},{8,0},{9,1},... | collective-permute-start | bytes 786440 | tf_op jit(solution)/shard_map/ppermute | solution.py:88
  1.2 0.0 copy-start.3
  1.2 1.2 %begin.1 = (s32[8]{0:T(128)S(4)}, f32[1,8,8192]{2,1,0:T(8,128)S(1)}, f32[8,8192]{1,0:T(8,128)S(1)}, f32[8,8192]{1,0:T(8,128)S(1)}) custom-call(s32[8]{0:T(128)} %refs_0_.1, f32[1,8,8192]{2,1,0:T(8,128)} %refs_1_.1, f32[8,8192]{1,0:T(8,128)} %refs_2_.1, f32[8,8192]{1,0:T(8,128)} %refs_3_.1), custom_call_target="tpu_custom_call" | custom-call | tf_op jit(solution)/shard_map/begin/pallas_call | solution.py:36
  2.3 0.0 copy-done.3
  2.3 0.2 %collective-permute-done.other = f32[8,8192]{1,0:T(8,128)S(1)} collective-permute-done((f32[8,8192]{1,0:T(8,128)}, f32[8,8192]{1,0:T(8,128)S(1)}, u32[]{:S(2)}, u32[]{:S(2)}) %collective-permute-start) | collective-permute-done | bytes 262176 | tf_op jit(solution)/shard_map/ppermute | solution.py:88
  2.5 0.0 copy-start
  2.5 0.0 copy-start.1
  2.5 0.1 rows_kernel.1
  2.6 0.0 copy-start.2
  2.7 2.7 %collective-permute-start.1 = (f32[64,128]{1,0:T(8,128)S(1)}, f32[64,128]{1,0:T(8,128)S(1)}, u32[]{:S(2)}, u32[]{:S(2)}) collective-permute-start(f32[64,128]{1,0:T(8,128)S(1)} %get-tuple-element.56), channel_id=1, source_target_pairs={{0,24},{1,25},{2,26},{3,27},{4,28},{5,29},{6,30},{7,31},{8,18},{9,... | collective-permute-start | bytes 98312 | tf_op jit(solution)/shard_map/ppermute | solution.py:108
  5.3 1.4 %collective-permute-start.3 = (f32[64,128]{1,0:T(8,128)S(1)}, f32[64,128]{1,0:T(8,128)S(1)}, u32[]{:S(2)}, u32[]{:S(2)}) collective-permute-start(f32[64,128]{1,0:T(8,128)S(1)} %get-tuple-element.55), channel_id=1, source_target_pairs={{0,10},{1,11},{2,8},{3,9},{4,14},{5,15},{6,12},{7,13},{8,2},{9,3},... | collective-permute-start | bytes 98312 | tf_op jit(solution)/shard_map/ppermute | solution.py:88
  6.8 0.0 copy-done
  6.8 0.0 copy-done.1
  6.8 0.0 copy-done.2
  6.8 1.0 %divide_subtract_fusion = (f32[1,8,8192]{2,1,0:T(8,128)S(1)}, f32[1,8,8192]{2,1,0:T(8,128)}, f32[1,8,8192]{2,1,0:T(8,128)}) fusion(f32[1,8,8192]{2,1,0:T(8,128)S(1)} %get-tuple-element.34.inner, f32[8]{0:T(128)S(1)} %get-tuple-element.60, f32[8]{0:T(128)S(1)} %get-tuple-element.59, bf16[1,8,8192]{2,1,0:T(8,128)(2,1)S(1)} %copy-done.2, ...), kind=kLoop, calls=%fused_computation.5 | loop fusion | flops 983040 | bytes 1704000 | tf_op jit(solution)/shard_map/sub | solution.py:209
  7.8 0.0 collective-permute-done.1
  7.8 0.5 %collective-permute-start.2 = (f32[64,128]{1,0:T(8,128)S(1)}, f32[64,128]{1,0:T(8,128)S(1)}, u32[]{:S(2)}, u32[]{:S(2)}) collective-permute-start(f32[64,128]{1,0:T(8,128)S(1)} %collective-permute-done.1), channel_id=1, source_target_pairs={{0,8},{1,9},{2,10},{3,11},{4,12},{5,13},{6,14},{7,15},{8,0},{9,1},... | collective-permute-start | bytes 98312 | tf_op jit(solution)/shard_map/ppermute | solution.py:88
  8.3 0.1 fusion.2
  8.4 0.3 %collective-permute-done.3 = f32[64,128]{1,0:T(8,128)S(1)} collective-permute-done((f32[64,128]{1,0:T(8,128)S(1)}, f32[64,128]{1,0:T(8,128)S(1)}, u32[]{:S(2)}, u32[]{:S(2)}) %collective-permute-start.3) | collective-permute-done | bytes 32800 | tf_op jit(solution)/shard_map/ppermute | solution.py:88
  8.7 0.5 %collective-permute-done.2 = f32[64,128]{1,0:T(8,128)S(1)} collective-permute-done((f32[64,128]{1,0:T(8,128)S(1)}, f32[64,128]{1,0:T(8,128)S(1)}, u32[]{:S(2)}, u32[]{:S(2)}) %collective-permute-start.2) | collective-permute-done | bytes 32800 | tf_op jit(solution)/shard_map/ppermute | solution.py:88
  9.2 3.1 %collective-permute-start.4 = (bf16[2,64,128]{2,1,0:T(8,128)(2,1)S(1)}, bf16[2,64,128]{2,1,0:T(8,128)(2,1)S(1)}, u32[]{:S(2)}, u32[]{:S(2)}) collective-permute-start(bf16[2,64,128]{2,1,0:T(8,128)(2,1)S(1)} %pad_maximum_fusion.own), channel_id=1, source_target_pairs={{0,12},{1,13},{2,14},{3,15},{4,9},{5,8},{6,11},{7,10},{8,5},{9,4},... | collective-permute-start | bytes 98312 | tf_op jit(solution)/shard_map/ppermute | solution.py:108
  12.4 0.8 %collective-permute-start.6 = (bf16[2,64,128]{2,1,0:T(8,128)(2,1)S(1)}, bf16[2,64,128]{2,1,0:T(8,128)(2,1)S(1)}, u32[]{:S(2)}, u32[]{:S(2)}) collective-permute-start(bf16[2,64,128]{2,1,0:T(8,128)(2,1)S(1)} %pad_maximum_fusion.own), channel_id=1, source_target_pairs={{0,9},{1,8},{2,11},{3,10},{4,13},{5,12},{6,15},{7,14},{8,1},{9,0},... | collective-permute-start | bytes 98312 | tf_op jit(solution)/shard_map/ppermute | solution.py:88
  13.2 0.9 %broadcast_select_fusion = (f32[8,8192]{1,0:T(8,128)}, f32[8,8192]{1,0:T(8,128)}) fusion(f32[8,8192]{1,0:T(8,128)S(1)} %get-tuple-element.44.moment, f32[8192]{0:T(1024)S(1)} %add_bitcast_fusion, pred[8]{0:T(512)(128)(4,1)S(1)} %fusion.2, f32[8,8192]{1,0:T(8,128)S(1)} %get-tuple-element.42.outer, f32[8192]{0:T(1024)S(1)} %bitcast.12), kind=kLoop, calls=%fused_computation.6 | loop fusion | flops 131072 | bytes 1114120 | tf_op jit(solution)/shard_map/jit(_where)/select_n | solution.py:184
  14.1 0.0 collective-permute-done.4.got
  14.2 1.2 %collective-permute-start.5 = (bf16[2,64,128]{2,1,0:T(8,128)(2,1)S(1)}, bf16[2,64,128]{2,1,0:T(8,128)(2,1)S(1)}, u32[]{:S(2)}, u32[]{:S(2)}) collective-permute-start(bf16[2,64,128]{2,1,0:T(8,128)(2,1)S(1)} %collective-permute-done.4.got), channel_id=1, source_target_pairs={{0,8},{1,9},{2,10},{3,11},{4,12},{5,13},{6,14},{7,15},{8,0},{9,1},... | collective-permute-start | bytes 98312 | tf_op jit(solution)/shard_map/ppermute | solution.py:88
  15.3 0.8 %add_select_fusion = f32[1,8,8192]{2,1,0:T(8,128)} fusion(f32[1,8,8192]{2,1,0:T(8,128)S(1)} %get-tuple-element.40, f32[8192]{0:T(1024)S(1)} %multiply_bitcast_fusion, pred[8]{0:T(512)(128)(4,1)S(1)} %fusion.2), kind=kLoop, calls=%fused_computation.4 | loop fusion | flops 196608 | bytes 557064 | tf_op jit(solution)/shard_map/jit(_where)/select_n | solution.py:233
  16.1 0.0 collective-permute-done.6.across_1
  16.1 0.1 collective-permute-done.5.other
  16.2 0.7 %order.1 = bf16[512,128]{1,0:T(8,128)(2,1)} custom-call(bf16[2,64,128]{2,1,0:T(8,128)(2,1)S(1)} %pad_maximum_fusion.own, bf16[2,64,128]{2,1,0:T(8,128)(2,1)S(1)} %collective-permute-done.6.across_1, bf16[2,64,128]{2,1,0:T(8,128)(2,1)S(1)} %collective-permute-done.4.got, bf16[2,64,128]{2,1,0:T(8,128)(2,1)S(1)} %collective-permute-done.5.other), custom_call_target="tpu_custom_call" | custom-call | tf_op jit(solution)/shard_map/order/pallas_call | solution.py:148
  (7 shorter events, 0.1 us)
Async XLA Ops:
  0.6 1.9 %collective-permute-start = (f32[8,8192]{1,0:T(8,128)}, f32[8,8192]{1,0:T(8,128)S(1)}, u32[]{:S(2)}, u32[]{:S(2)}) collective-permute-start(f32[8,8192]{1,0:T(8,128)} %bitcast.11), channel_id=1, source_target_pairs={{0,8},{1,9},{2,10},{3,11},{4,12},{5,13},{6,14},{7,15},{8,0},{9,1},... | collective-permute-start | bytes 786440 | tf_op jit(solution)/shard_map/ppermute | solution.py:88
  1.2 1.2 %copy-start.3 = (s32[8]{0:T(128)S(1)}, s32[8]{0:T(128)}, u32[]{:S(2)}) copy-start(s32[8]{0:T(128)} %param.9) | copy-start | bytes 100
  2.5 4.2 %copy-start = (f32[1,8,8192]{2,1,0:T(8,128)S(1)}, f32[1,8,8192]{2,1,0:T(8,128)}, u32[]{:S(2)}) copy-start(f32[1,8,8192]{2,1,0:T(8,128)} %param.12) | copy-start | bytes 786436
  2.5 4.2 %copy-start.1 = (f32[1,8,8192]{2,1,0:T(8,128)S(1)}, f32[1,8,8192]{2,1,0:T(8,128)}, u32[]{:S(2)}) copy-start(f32[1,8,8192]{2,1,0:T(8,128)} %param.13) | copy-start | bytes 786436
  2.6 4.1 %copy-start.2 = (bf16[1,8,8192]{2,1,0:T(8,128)(2,1)S(1)}, bf16[1,8,8192]{2,1,0:T(8,128)(2,1)}, u32[]{:S(2)}) copy-start(bf16[1,8,8192]{2,1,0:T(8,128)(2,1)} %param.11) | copy-start | bytes 393220
  2.7 5.1 %collective-permute-start.1 = (f32[64,128]{1,0:T(8,128)S(1)}, f32[64,128]{1,0:T(8,128)S(1)}, u32[]{:S(2)}, u32[]{:S(2)}) collective-permute-start(f32[64,128]{1,0:T(8,128)S(1)} %get-tuple-element.56), channel_id=1, source_target_pairs={{0,24},{1,25},{2,26},{3,27},{4,28},{5,29},{6,30},{7,31},{8,18},{9,... | collective-permute-start | bytes 98312 | tf_op jit(solution)/shard_map/ppermute | solution.py:108
  5.3 3.4 %collective-permute-start.3 = (f32[64,128]{1,0:T(8,128)S(1)}, f32[64,128]{1,0:T(8,128)S(1)}, u32[]{:S(2)}, u32[]{:S(2)}) collective-permute-start(f32[64,128]{1,0:T(8,128)S(1)} %get-tuple-element.55), channel_id=1, source_target_pairs={{0,10},{1,11},{2,8},{3,9},{4,14},{5,15},{6,12},{7,13},{8,2},{9,3},... | collective-permute-start | bytes 98312 | tf_op jit(solution)/shard_map/ppermute | solution.py:88
  7.8 1.4 %collective-permute-start.2 = (f32[64,128]{1,0:T(8,128)S(1)}, f32[64,128]{1,0:T(8,128)S(1)}, u32[]{:S(2)}, u32[]{:S(2)}) collective-permute-start(f32[64,128]{1,0:T(8,128)S(1)} %collective-permute-done.1), channel_id=1, source_target_pairs={{0,8},{1,9},{2,10},{3,11},{4,12},{5,13},{6,14},{7,15},{8,0},{9,1},... | collective-permute-start | bytes 98312 | tf_op jit(solution)/shard_map/ppermute | solution.py:88
  9.2 4.9 %collective-permute-start.4 = (bf16[2,64,128]{2,1,0:T(8,128)(2,1)S(1)}, bf16[2,64,128]{2,1,0:T(8,128)(2,1)S(1)}, u32[]{:S(2)}, u32[]{:S(2)}) collective-permute-start(bf16[2,64,128]{2,1,0:T(8,128)(2,1)S(1)} %pad_maximum_fusion.own), channel_id=1, source_target_pairs={{0,12},{1,13},{2,14},{3,15},{4,9},{5,8},{6,11},{7,10},{8,5},{9,4},... | collective-permute-start | bytes 98312 | tf_op jit(solution)/shard_map/ppermute | solution.py:108
  12.4 3.7 %collective-permute-start.6 = (bf16[2,64,128]{2,1,0:T(8,128)(2,1)S(1)}, bf16[2,64,128]{2,1,0:T(8,128)(2,1)S(1)}, u32[]{:S(2)}, u32[]{:S(2)}) collective-permute-start(bf16[2,64,128]{2,1,0:T(8,128)(2,1)S(1)} %pad_maximum_fusion.own), channel_id=1, source_target_pairs={{0,9},{1,8},{2,11},{3,10},{4,13},{5,12},{6,15},{7,14},{8,1},{9,0},... | collective-permute-start | bytes 98312 | tf_op jit(solution)/shard_map/ppermute | solution.py:88
  14.2 2.0 %collective-permute-start.5 = (bf16[2,64,128]{2,1,0:T(8,128)(2,1)S(1)}, bf16[2,64,128]{2,1,0:T(8,128)(2,1)S(1)}, u32[]{:S(2)}, u32[]{:S(2)}) collective-permute-start(bf16[2,64,128]{2,1,0:T(8,128)(2,1)S(1)} %collective-permute-done.4.got), channel_id=1, source_target_pairs={{0,8},{1,9},{2,10},{3,11},{4,12},{5,13},{6,14},{7,15},{8,0},{9,1},... | collective-permute-start | bytes 98312 | tf_op jit(solution)/shard_map/ppermute | solution.py:88

commit v6 on v5

--- a/solution.py
+++ b/solution.py
@@ -120,7 +120,8 @@
 
 def order_kernel(own, across_1, got, other, refreshed, sems):
     core = lax.axis_index("replica") % 2
-    four, one = (lax.axis_index("fsdp") // 4) % 2, lax.axis_index("fsdp") % 2
+    shard = lax.axis_index("fsdp")
+    four, two, one = (shard // 4) % 2, (shard // 2) % 2, shard % 2
     straight = (core + four + 1) % 2
     far = ((one + 1 + straight) % 2, (one + straight) % 2)
     blocks, rows = own.shape[0], own.shape[1]
@@ -132,7 +133,7 @@
         (other, 1 - four, far[1]),
     ):
         for i in range(blocks):
-            place = ((i // 2 * 2 + at_4) * 2 + i % 2) * 2 + at_1
+            place = ((i // 2 * 2 + at_4) * 2 + (i + two) % 2) * 2 + at_1
             target = refreshed.at[pl.ds(pl.multiple_of(place * rows, rows), rows), :]
             copies.append(pltpu.make_async_copy(source.at[i], target, sems.at[len(copies)]))
     for copy in copies:
@@ -215,7 +216,7 @@
     new_outer_row = part(drift) + part(drift_across)
     refreshed_shard = new_outer_row.astype(jnp.bfloat16)
     next_shard = (near_across + far_across).astype(jnp.bfloat16)
-    held = jnp.stack(in_order(bit_of("fsdp", 2), refreshed_shard, next_shard))
+    held = jnp.stack((refreshed_shard, next_shard))
     bit = 8
     while bit < lax.axis_size("fsdp"):
         held = jnp.stack(in_order(bit_of("fsdp", bit), held, swap(held, 1, bit)))

time: 17 us -> 17 us (level)
  no operation moved by 1% of the time
where the time goes in v6:
time: 17 us; the launch traced here: 16.9 us
  starting transfers between devices  10.3 us (61%)
  other arithmetic  2.87 us (17%)
  Pallas kernels  1.96 us (12%)
  waiting for transfers between devices  1 us (6%)
  between operations  0.7 us (4%)
    ppermute x2, starting transfers between devices, ring(): got = lax.ppermute(far, AXES, pairs)  5.81 us
    ppermute x5, starting transfers between devices, swap(): return lax.ppermute(block, AXES, pairs)  4.52 us
    pallas_call x1, Pallas kernels, begin(): pl.pallas_call(begin_kernel, out_shape=[memory(x.shape, x.dtype) for memo...  1.16 us
    sub x1, other arithmetic, on_device(): inner_params * (1.0 - inner_rate * decay_rate)  1.01 us
    ppermute x5, waiting for transfers between devices, swap(): return lax.ppermute(block, AXES, pairs)  0.99 us
    select_n x1, other arithmetic, put_row(): return jnp.where(chosen, row.reshape(1, width), table)  0.9 us
    select_n x1, other arithmetic, on_device(): new_inner = jnp.where(chosen[None], blended, stepped)  0.79 us
    pallas_call x1, Pallas kernels, put_in_order(): pl.pallas_call(order_kernel, out_shape=jax.ShapeDtypeStruct((count * rows...  0.71 us
  transfers between devices with their start and end apart: 7, of which 4 were waited for; matrix products, arithmetic and copies ran while one was open for 17% of the time, Pallas kernels for 7%

profile of v6, /device:TPU:0, one launch (start us, length us, event | category | flops | bytes accessed | tf_op | source)
XLA Modules:
  0.0 16.9 jit_solution(10209980977857361207)
XLA Ops:
  0.6 0.5 %collective-permute-start = (f32[8,8192]{1,0:T(8,128)}, f32[8,8192]{1,0:T(8,128)S(1)}, u32[]{:S(2)}, u32[]{:S(2)}) collective-permute-start(f32[8,8192]{1,0:T(8,128)} %bitcast.10), channel_id=1, source_target_pairs={{0,8},{1,9},{2,10},{3,11},{4,12},{5,13},{6,14},{7,15},{8,0},{9,1},... | collective-permute-start | bytes 786440 | tf_op jit(solution)/shard_map/ppermute | solution.py:88
  1.2 0.0 copy-start.3
  1.2 1.2 %begin.1 = (s32[8]{0:T(128)S(4)}, f32[1,8,8192]{2,1,0:T(8,128)S(1)}, f32[8,8192]{1,0:T(8,128)S(1)}, f32[8,8192]{1,0:T(8,128)S(1)}) custom-call(s32[8]{0:T(128)} %refs_0_.1, f32[1,8,8192]{2,1,0:T(8,128)} %refs_1_.1, f32[8,8192]{1,0:T(8,128)} %refs_2_.1, f32[8,8192]{1,0:T(8,128)} %refs_3_.1), custom_call_target="tpu_custom_call" | custom-call | tf_op jit(solution)/shard_map/begin/pallas_call | solution.py:36
  2.3 0.0 copy-done.3
  2.3 0.2 %collective-permute-done.other = f32[8,8192]{1,0:T(8,128)S(1)} collective-permute-done((f32[8,8192]{1,0:T(8,128)}, f32[8,8192]{1,0:T(8,128)S(1)}, u32[]{:S(2)}, u32[]{:S(2)}) %collective-permute-start) | collective-permute-done | bytes 262176 | tf_op jit(solution)/shard_map/ppermute | solution.py:88
  2.5 0.0 copy-start
  2.5 0.0 copy-start.1
  2.5 0.1 rows_kernel.1
  2.6 0.0 copy-start.2
  2.7 2.7 %collective-permute-start.1 = (f32[64,128]{1,0:T(8,128)S(1)}, f32[64,128]{1,0:T(8,128)S(1)}, u32[]{:S(2)}, u32[]{:S(2)}) collective-permute-start(f32[64,128]{1,0:T(8,128)S(1)} %get-tuple-element.56), channel_id=1, source_target_pairs={{0,24},{1,25},{2,26},{3,27},{4,28},{5,29},{6,30},{7,31},{8,18},{9,... | collective-permute-start | bytes 98312 | tf_op jit(solution)/shard_map/ppermute | solution.py:108
  5.3 1.4 %collective-permute-start.3 = (f32[64,128]{1,0:T(8,128)S(1)}, f32[64,128]{1,0:T(8,128)S(1)}, u32[]{:S(2)}, u32[]{:S(2)}) collective-permute-start(f32[64,128]{1,0:T(8,128)S(1)} %get-tuple-element.55), channel_id=1, source_target_pairs={{0,10},{1,11},{2,8},{3,9},{4,14},{5,15},{6,12},{7,13},{8,2},{9,3},... | collective-permute-start | bytes 98312 | tf_op jit(solution)/shard_map/ppermute | solution.py:88
  6.8 0.0 copy-done
  6.8 0.0 copy-done.1
  6.8 0.0 copy-done.2
  6.8 1.0 %divide_subtract_fusion = (f32[1,8,8192]{2,1,0:T(8,128)S(1)}, f32[1,8,8192]{2,1,0:T(8,128)}, f32[1,8,8192]{2,1,0:T(8,128)}) fusion(f32[1,8,8192]{2,1,0:T(8,128)S(1)} %get-tuple-element.34.inner, f32[8]{0:T(128)S(1)} %get-tuple-element.60, f32[8]{0:T(128)S(1)} %get-tuple-element.59, bf16[1,8,8192]{2,1,0:T(8,128)(2,1)S(1)} %copy-done.2, ...), kind=kLoop, calls=%fused_computation.5 | loop fusion | flops 983040 | bytes 1704000 | tf_op jit(solution)/shard_map/sub | solution.py:210
  7.8 0.0 collective-permute-done.1
  7.8 0.5 %collective-permute-start.2 = (f32[64,128]{1,0:T(8,128)S(1)}, f32[64,128]{1,0:T(8,128)S(1)}, u32[]{:S(2)}, u32[]{:S(2)}) collective-permute-start(f32[64,128]{1,0:T(8,128)S(1)} %collective-permute-done.1), channel_id=1, source_target_pairs={{0,8},{1,9},{2,10},{3,11},{4,12},{5,13},{6,14},{7,15},{8,0},{9,1},... | collective-permute-start | bytes 98312 | tf_op jit(solution)/shard_map/ppermute | solution.py:88
  8.3 0.1 fusion.3
  8.4 0.3 %collective-permute-done.3 = f32[64,128]{1,0:T(8,128)S(1)} collective-permute-done((f32[64,128]{1,0:T(8,128)S(1)}, f32[64,128]{1,0:T(8,128)S(1)}, u32[]{:S(2)}, u32[]{:S(2)}) %collective-permute-start.3) | collective-permute-done | bytes 32800 | tf_op jit(solution)/shard_map/ppermute | solution.py:88
  8.7 0.5 %collective-permute-done.2 = f32[64,128]{1,0:T(8,128)S(1)} collective-permute-done((f32[64,128]{1,0:T(8,128)S(1)}, f32[64,128]{1,0:T(8,128)S(1)}, u32[]{:S(2)}, u32[]{:S(2)}) %collective-permute-start.2) | collective-permute-done | bytes 32800 | tf_op jit(solution)/shard_map/ppermute | solution.py:88
  9.2 3.1 %collective-permute-start.4 = (bf16[2,64,128]{2,1,0:T(8,128)(2,1)S(1)}, bf16[2,64,128]{2,1,0:T(8,128)(2,1)S(1)}, u32[]{:S(2)}, u32[]{:S(2)}) collective-permute-start(bf16[2,64,128]{2,1,0:T(8,128)(2,1)S(1)} %pad_maximum_fusion.own), channel_id=1, source_target_pairs={{0,12},{1,13},{2,14},{3,15},{4,9},{5,8},{6,11},{7,10},{8,5},{9,4},... | collective-permute-start | bytes 98312 | tf_op jit(solution)/shard_map/ppermute | solution.py:108
  12.4 0.8 %collective-permute-start.6 = (bf16[2,64,128]{2,1,0:T(8,128)(2,1)S(1)}, bf16[2,64,128]{2,1,0:T(8,128)(2,1)S(1)}, u32[]{:S(2)}, u32[]{:S(2)}) collective-permute-start(bf16[2,64,128]{2,1,0:T(8,128)(2,1)S(1)} %pad_maximum_fusion.own), channel_id=1, source_target_pairs={{0,9},{1,8},{2,11},{3,10},{4,13},{5,12},{6,15},{7,14},{8,1},{9,0},... | collective-permute-start | bytes 98312 | tf_op jit(solution)/shard_map/ppermute | solution.py:88
  13.2 0.9 %broadcast_select_fusion = (f32[8,8192]{1,0:T(8,128)}, f32[8,8192]{1,0:T(8,128)}) fusion(f32[8,8192]{1,0:T(8,128)S(1)} %get-tuple-element.44.moment, f32[8192]{0:T(1024)S(1)} %get-tuple-element.53, pred[8]{0:T(512)(128)(4,1)S(1)} %fusion.3, f32[8,8192]{1,0:T(8,128)S(1)} %get-tuple-element.42.outer, f32[8192]{0:T(1024)S(1)} %bitcast.12), kind=kLoop, calls=%fused_computation.6 | loop fusion | flops 131072 | bytes 1114120 | tf_op jit(solution)/shard_map/jit(_where)/select_n | solution.py:185
  14.1 0.0 collective-permute-done.4.got
  14.1 1.2 %collective-permute-start.5 = (bf16[2,64,128]{2,1,0:T(8,128)(2,1)S(1)}, bf16[2,64,128]{2,1,0:T(8,128)(2,1)S(1)}, u32[]{:S(2)}, u32[]{:S(2)}) collective-permute-start(bf16[2,64,128]{2,1,0:T(8,128)(2,1)S(1)} %collective-permute-done.4.got), channel_id=1, source_target_pairs={{0,8},{1,9},{2,10},{3,11},{4,12},{5,13},{6,14},{7,15},{8,0},{9,1},... | collective-permute-start | bytes 98312 | tf_op jit(solution)/shard_map/ppermute | solution.py:88
  15.3 0.8 %add_select_fusion = f32[1,8,8192]{2,1,0:T(8,128)} fusion(f32[1,8,8192]{2,1,0:T(8,128)S(1)} %get-tuple-element.40, f32[8192]{0:T(1024)S(1)} %multiply_bitcast_fusion, pred[8]{0:T(512)(128)(4,1)S(1)} %fusion.3), kind=kLoop, calls=%fused_computation.4 | loop fusion | flops 196608 | bytes 557064 | tf_op jit(solution)/shard_map/jit(_where)/select_n | solution.py:234
  16.1 0.0 collective-permute-done.6.across_1
  16.1 0.1 collective-permute-done.5.other
  16.2 0.7 %order.1 = bf16[512,128]{1,0:T(8,128)(2,1)} custom-call(bf16[2,64,128]{2,1,0:T(8,128)(2,1)S(1)} %pad_maximum_fusion.own, bf16[2,64,128]{2,1,0:T(8,128)(2,1)S(1)} %collective-permute-done.6.across_1, bf16[2,64,128]{2,1,0:T(8,128)(2,1)S(1)} %collective-permute-done.4.got, bf16[2,64,128]{2,1,0:T(8,128)(2,1)S(1)} %collective-permute-done.5.other), custom_call_target="tpu_custom_call" | custom-call | tf_op jit(solution)/shard_map/order/pallas_call | solution.py:149
  (5 shorter events, 0.1 us)
Async XLA Ops:
  0.6 1.9 %collective-permute-start = (f32[8,8192]{1,0:T(8,128)}, f32[8,8192]{1,0:T(8,128)S(1)}, u32[]{:S(2)}, u32[]{:S(2)}) collective-permute-start(f32[8,8192]{1,0:T(8,128)} %bitcast.10), channel_id=1, source_target_pairs={{0,8},{1,9},{2,10},{3,11},{4,12},{5,13},{6,14},{7,15},{8,0},{9,1},... | collective-permute-start | bytes 786440 | tf_op jit(solution)/shard_map/ppermute | solution.py:88
  1.2 1.2 %copy-start.3 = (s32[8]{0:T(128)S(1)}, s32[8]{0:T(128)}, u32[]{:S(2)}) copy-start(s32[8]{0:T(128)} %param.9) | copy-start | bytes 100
  2.5 4.2 %copy-start = (f32[1,8,8192]{2,1,0:T(8,128)S(1)}, f32[1,8,8192]{2,1,0:T(8,128)}, u32[]{:S(2)}) copy-start(f32[1,8,8192]{2,1,0:T(8,128)} %param.12) | copy-start | bytes 786436
  2.5 4.2 %copy-start.1 = (f32[1,8,8192]{2,1,0:T(8,128)S(1)}, f32[1,8,8192]{2,1,0:T(8,128)}, u32[]{:S(2)}) copy-start(f32[1,8,8192]{2,1,0:T(8,128)} %param.13) | copy-start | bytes 786436
  2.6 4.1 %copy-start.2 = (bf16[1,8,8192]{2,1,0:T(8,128)(2,1)S(1)}, bf16[1,8,8192]{2,1,0:T(8,128)(2,1)}, u32[]{:S(2)}) copy-start(bf16[1,8,8192]{2,1,0:T(8,128)(2,1)} %param.11) | copy-start | bytes 393220
  2.7 5.1 %collective-permute-start.1 = (f32[64,128]{1,0:T(8,128)S(1)}, f32[64,128]{1,0:T(8,128)S(1)}, u32[]{:S(2)}, u32[]{:S(2)}) collective-permute-start(f32[64,128]{1,0:T(8,128)S(1)} %get-tuple-element.56), channel_id=1, source_target_pairs={{0,24},{1,25},{2,26},{3,27},{4,28},{5,29},{6,30},{7,31},{8,18},{9,... | collective-permute-start | bytes 98312 | tf_op jit(solution)/shard_map/ppermute | solution.py:108
  5.3 3.4 %collective-permute-start.3 = (f32[64,128]{1,0:T(8,128)S(1)}, f32[64,128]{1,0:T(8,128)S(1)}, u32[]{:S(2)}, u32[]{:S(2)}) collective-permute-start(f32[64,128]{1,0:T(8,128)S(1)} %get-tuple-element.55), channel_id=1, source_target_pairs={{0,10},{1,11},{2,8},{3,9},{4,14},{5,15},{6,12},{7,13},{8,2},{9,3},... | collective-permute-start | bytes 98312 | tf_op jit(solution)/shard_map/ppermute | solution.py:88
  7.8 1.4 %collective-permute-start.2 = (f32[64,128]{1,0:T(8,128)S(1)}, f32[64,128]{1,0:T(8,128)S(1)}, u32[]{:S(2)}, u32[]{:S(2)}) collective-permute-start(f32[64,128]{1,0:T(8,128)S(1)} %collective-permute-done.1), channel_id=1, source_target_pairs={{0,8},{1,9},{2,10},{3,11},{4,12},{5,13},{6,14},{7,15},{8,0},{9,1},... | collective-permute-start | bytes 98312 | tf_op jit(solution)/shard_map/ppermute | solution.py:88
  9.2 4.9 %collective-permute-start.4 = (bf16[2,64,128]{2,1,0:T(8,128)(2,1)S(1)}, bf16[2,64,128]{2,1,0:T(8,128)(2,1)S(1)}, u32[]{:S(2)}, u32[]{:S(2)}) collective-permute-start(bf16[2,64,128]{2,1,0:T(8,128)(2,1)S(1)} %pad_maximum_fusion.own), channel_id=1, source_target_pairs={{0,12},{1,13},{2,14},{3,15},{4,9},{5,8},{6,11},{7,10},{8,5},{9,4},... | collective-permute-start | bytes 98312 | tf_op jit(solution)/shard_map/ppermute | solution.py:108
  12.4 3.7 %collective-permute-start.6 = (bf16[2,64,128]{2,1,0:T(8,128)(2,1)S(1)}, bf16[2,64,128]{2,1,0:T(8,128)(2,1)S(1)}, u32[]{:S(2)}, u32[]{:S(2)}) collective-permute-start(bf16[2,64,128]{2,1,0:T(8,128)(2,1)S(1)} %pad_maximum_fusion.own), channel_id=1, source_target_pairs={{0,9},{1,8},{2,11},{3,10},{4,13},{5,12},{6,15},{7,14},{8,1},{9,0},... | collective-permute-start | bytes 98312 | tf_op jit(solution)/shard_map/ppermute | solution.py:88
  14.1 2.0 %collective-permute-start.5 = (bf16[2,64,128]{2,1,0:T(8,128)(2,1)S(1)}, bf16[2,64,128]{2,1,0:T(8,128)(2,1)S(1)}, u32[]{:S(2)}, u32[]{:S(2)}) collective-permute-start(bf16[2,64,128]{2,1,0:T(8,128)(2,1)S(1)} %collective-permute-done.4.got), channel_id=1, source_target_pairs={{0,8},{1,9},{2,10},{3,11},{4,12},{5,13},{6,14},{7,15},{8,0},{9,1},... | collective-permute-start | bytes 98312 | tf_op jit(solution)/shard_map/ppermute | solution.py:88

commit v7 on v6

--- a/solution.py
+++ b/solution.py
@@ -20,7 +20,7 @@
 
 
 def begin_kernel(*refs):
-    sources, targets, sems = refs[:4], refs[4:8], refs[8]
+    sources, targets, sems = refs[:5], refs[5:10], refs[10]
     copies = [
         pltpu.make_async_copy(source, target, sems.at[i])
         for i, (source, target) in enumerate(zip(sources, targets))
@@ -32,13 +32,13 @@
 
 
 def begin(*arrays):
-    memories = (pltpu.SMEM,) + (pltpu.VMEM,) * 3
+    memories = (pltpu.SMEM,) + (pltpu.VMEM,) * 4
     return pl.pallas_call(
         begin_kernel,
         out_shape=[memory(x.shape, x.dtype) for memory, x in zip(memories, arrays)],
-        in_specs=[pl.BlockSpec(memory_space=pl.ANY)] * 4,
+        in_specs=[pl.BlockSpec(memory_space=pl.ANY)] * 5,
         out_specs=[pl.BlockSpec(memory_space=memory) for memory in memories],
-        scratch_shapes=[pltpu.SemaphoreType.DMA((4,))],
+        scratch_shapes=[pltpu.SemaphoreType.DMA((5,))],
         name="begin",
     )(*arrays)
 
@@ -54,16 +54,19 @@
         folded[pl.ds(top, SUBLANES), :] = tile
 
 
-def rows_kernel(index, outer, inner, other, moment, drift, share, moment_row, chosen):
-    def drifts(at):
-        return (outer[:, at] - inner[0, :, at]) + (outer[:, at] - other[:, at])
-
-    fold(drifts, index[0], drift)
+def rows_kernel(index, outer, moment, share, moment_row, chosen):
     fold(lambda at: moment[:, at], index[0], moment_row)
     fold(lambda at: outer[:, at], index[0], share)
     share[...] = 0.5 * (share[...] - outer_rate * momentum_keep * momentum_keep * moment_row[...])
     sublane = lax.broadcasted_iota(jnp.int32, chosen.shape, 0)
     chosen[...] = (sublane == index[0]).astype(jnp.int32)
+
+
+def drift_kernel(index, outer, inner, other, drift):
+    def drifts(at):
+        return (outer[:, at] - inner[0, :, at]) + (outer[:, at] - other[:, at])
+
+    fold(drifts, index[0], drift)
 
 
 def in_fast_memory(kernel, index, tables, shapes):
@@ -169,21 +172,19 @@
     replicas = lax.axis_size("replica")
     frags, width = outer_params.shape
     other_inner = swap(inner_params[0], 1, 0)
-    index, inner_params, outer_params, outer_momentum = begin(
-        frag_index, inner_params, outer_params, outer_momentum
+    index, inner_params, outer_params, outer_momentum, inner_step = begin(
+        frag_index, inner_params, outer_params, outer_momentum, inner_step
     )
     row = ((width // LANES, LANES), jnp.float32)
-    drift, share, moment_row, chosen = in_fast_memory(
+    share, moment_row, chosen = in_fast_memory(
         rows_kernel,
         index,
-        (outer_params, inner_params, other_inner, outer_momentum),
-        (row, row, row, ((frags, LANES), jnp.int32)),
-    )
-    chosen = chosen[:, :1] != 0
-
-    def put_row(row, table):
-        return jnp.where(chosen, row.reshape(1, width), table)
-
+        (outer_params, outer_momentum),
+        (row, row, ((frags, LANES), jnp.int32)),
+    )
+    (drift,) = in_fast_memory(
+        drift_kernel, index, (outer_params, inner_params, other_inner), (row,)
+    )
     half = replicas // 2
     bit = 2
     while bit < half:
@@ -198,9 +199,7 @@
     got, other, near_across, is_a = ring(part(drift), far, half, (0, 2))
     drift_across, far_across = jnp.where(is_a, got, other), jnp.where(is_a, other, got)
 
-    inner_params, outer_params, outer_momentum = after(
-        (inner_params, outer_params, outer_momentum), far
-    )
+    inner_params, inner_step = after((inner_params, inner_step), far)
     step_count = inner_step.astype(jnp.float32)[None, :, None]
     grad_wide = grads.astype(jnp.float32)
     first_moment = beta_first * adam_first + (1.0 - beta_first) * grad_wide
@@ -224,9 +223,14 @@
     got, other, across_1, _ = ring(held, held, 0, (4, 1))
     refreshed = put_in_order(held, across_1, got, other)
 
-    stepped, refreshed_shard, outer_params, outer_momentum = after(
-        (stepped, refreshed_shard, outer_params, outer_momentum), held
-    )
+    stepped, refreshed_shard, chosen, outer_params, outer_momentum = after(
+        (stepped, refreshed_shard, chosen, outer_params, outer_momentum), held
+    )
+    chosen = chosen[:, :1] != 0
+
+    def put_row(row, table):
+        return jnp.where(chosen, row.reshape(1, width), table)
+
     new_outer = put_row(new_outer_row, outer_params)
     new_momentum = put_row(new_moment_row, outer_momentum)
     refreshed_row = refreshed_shard.astype(jnp.float32).reshape(1, 1, width)

time: 17 us -> 17 us (level)
  waiting for transfers between devices: 1 us -> 0.36 us
  starting transfers between devices: 10.3 us -> 10.9 us
    ppermute x5, waiting for transfers between devices: 0.99 us -> 0.21 us  [swap(): return lax.ppermute(block, AXES, pairs)]
    ppermute x5, starting transfers between devices: 4.52 us -> 5.27 us  [swap(): return lax.ppermute(block, AXES, pairs)]
  transfers between devices with their start and end apart: 7 -> 7, of which waited for: 4 -> 3; matrix products, arithmetic and copies ran while one was open for 17% -> 17% of each run, Pallas kernels for 7% -> 7%
where the time goes in v7:
time: 17 us; the launch traced here: 16.9 us
  starting transfers between devices  10.9 us (64%)
  other arithmetic  2.87 us (17%)
  Pallas kernels  1.98 us (12%)
  between operations  0.7 us (4%)
  waiting for transfers between devices  0.36 us (2%)
    ppermute x2, starting transfers between devices, ring(): got = lax.ppermute(far, AXES, pairs)  5.65 us
    ppermute x5, starting transfers between devices, swap(): return lax.ppermute(block, AXES, pairs)  5.27 us
    pallas_call x1, Pallas kernels, begin(): pl.pallas_call(begin_kernel, out_shape=[memory(x.shape, x.dtype) for memo...  1.15 us
    sub x1, other arithmetic, on_device(): inner_params * (1.0 - inner_rate * decay_rate)  1.01 us
    select_n x1, other arithmetic, put_row(): return jnp.where(chosen, row.reshape(1, width), table)  0.91 us
    select_n x1, other arithmetic, on_device(): new_inner = jnp.where(chosen[None], blended, stepped)  0.79 us
    pallas_call x1, Pallas kernels, put_in_order(): pl.pallas_call(order_kernel, out_shape=jax.ShapeDtypeStruct((count * rows...  0.71 us
  transfers between devices with their start and end apart: 7, of which 3 were waited for; matrix products, arithmetic and copies ran while one was open for 17% of the time, Pallas kernels for 7%

profile of v7, /device:TPU:0, one launch (start us, length us, event | category | flops | bytes accessed | tf_op | source)
XLA Modules:
  0.0 16.9 jit_solution(13004709029277577944)
XLA Ops:
  0.6 0.5 %collective-permute-start = (f32[8,8192]{1,0:T(8,128)}, f32[8,8192]{1,0:T(8,128)S(1)}, u32[]{:S(2)}, u32[]{:S(2)}) collective-permute-start(f32[8,8192]{1,0:T(8,128)} %bitcast.10), channel_id=1, source_target_pairs={{0,8},{1,9},{2,10},{3,11},{4,12},{5,13},{6,14},{7,15},{8,0},{9,1},... | collective-permute-start | bytes 786440 | tf_op jit(solution)/shard_map/ppermute | solution.py:91
  1.2 1.2 %begin.1 = (s32[8]{0:T(128)S(4)}, f32[1,8,8192]{2,1,0:T(8,128)S(1)}, f32[8,8192]{1,0:T(8,128)S(1)}, f32[8,8192]{1,0:T(8,128)S(1)}, s32[8]{0:T(128)S(1)}) custom-call(s32[8]{0:T(128)} %refs_0_.1, f32[1,8,8192]{2,1,0:T(8,128)} %refs_1_.1, f32[8,8192]{1,0:T(8,128)} %refs_2_.1, f32[8,8192]{1,0:T(8,128)} %refs_3_.1, s32[8]{0:T(128)} %refs_4_.1), custom_call_target="tpu_custom_call" | custom-call | tf_op jit(solution)/shard_map/begin/pallas_call | solution.py:36
  2.3 0.1 rows_kernel.1
  2.4 0.1 collective-permute-done.other
  2.5 0.0 copy-start
  2.5 0.0 copy-start.1
  2.5 0.1 drift_kernel.1
  2.6 0.0 copy-start.2
  2.6 2.7 %collective-permute-start.1 = (f32[64,128]{1,0:T(8,128)S(1)}, f32[64,128]{1,0:T(8,128)S(1)}, u32[]{:S(2)}, u32[]{:S(2)}) collective-permute-start(f32[64,128]{1,0:T(8,128)S(1)} %get-tuple-element.56), channel_id=1, source_target_pairs={{0,24},{1,25},{2,26},{3,27},{4,28},{5,29},{6,30},{7,31},{8,18},{9,... | collective-permute-start | bytes 98312 | tf_op jit(solution)/shard_map/ppermute | solution.py:111
  5.3 1.4 %collective-permute-start.3 = (f32[64,128]{1,0:T(8,128)S(1)}, f32[64,128]{1,0:T(8,128)S(1)}, u32[]{:S(2)}, u32[]{:S(2)}) collective-permute-start(f32[64,128]{1,0:T(8,128)S(1)} %get-tuple-element.55), channel_id=1, source_target_pairs={{0,10},{1,11},{2,8},{3,9},{4,14},{5,15},{6,12},{7,13},{8,2},{9,3},... | collective-permute-start | bytes 98312 | tf_op jit(solution)/shard_map/ppermute | solution.py:91
  6.7 0.1 collective-permute-done.1
  6.9 1.4 %collective-permute-start.2 = (f32[64,128]{1,0:T(8,128)S(1)}, f32[64,128]{1,0:T(8,128)S(1)}, u32[]{:S(2)}, u32[]{:S(2)}) collective-permute-start(f32[64,128]{1,0:T(8,128)S(1)} %collective-permute-done.1), channel_id=1, source_target_pairs={{0,8},{1,9},{2,10},{3,11},{4,12},{5,13},{6,14},{7,15},{8,0},{9,1},... | collective-permute-start | bytes 98312 | tf_op jit(solution)/shard_map/ppermute | solution.py:91
  8.3 0.0 copy-done
  8.3 0.0 copy-done.1
  8.3 0.0 copy-done.2
  8.3 1.0 %divide_subtract_fusion = (f32[1,8,8192]{2,1,0:T(8,128)S(1)}, f32[1,8,8192]{2,1,0:T(8,128)}, f32[1,8,8192]{2,1,0:T(8,128)}) fusion(f32[1,8,8192]{2,1,0:T(8,128)S(1)} %get-tuple-element.33.inner, f32[8]{0:T(128)S(1)} %get-tuple-element.60, f32[8]{0:T(128)S(1)} %get-tuple-element.59, bf16[1,8,8192]{2,1,0:T(8,128)(2,1)S(1)} %copy-done.2, ...), kind=kLoop, calls=%fused_computation.5 | loop fusion | flops 983040 | bytes 1704000 | tf_op jit(solution)/shard_map/sub | solution.py:209
  9.3 0.0 collective-permute-done.3
  9.3 0.0 collective-permute-done.2
  9.3 3.0 %collective-permute-start.4 = (bf16[2,64,128]{2,1,0:T(8,128)(2,1)S(1)}, bf16[2,64,128]{2,1,0:T(8,128)(2,1)S(1)}, u32[]{:S(2)}, u32[]{:S(2)}) collective-permute-start(bf16[2,64,128]{2,1,0:T(8,128)(2,1)S(1)} %pad_maximum_fusion.own), channel_id=1, source_target_pairs={{0,12},{1,13},{2,14},{3,15},{4,9},{5,8},{6,11},{7,10},{8,5},{9,4},... | collective-permute-start | bytes 98312 | tf_op jit(solution)/shard_map/ppermute | solution.py:111
  12.3 1.0 %collective-permute-start.6 = (bf16[2,64,128]{2,1,0:T(8,128)(2,1)S(1)}, bf16[2,64,128]{2,1,0:T(8,128)(2,1)S(1)}, u32[]{:S(2)}, u32[]{:S(2)}) collective-permute-start(bf16[2,64,128]{2,1,0:T(8,128)(2,1)S(1)} %pad_maximum_fusion.own), channel_id=1, source_target_pairs={{0,9},{1,8},{2,11},{3,10},{4,13},{5,12},{6,15},{7,14},{8,1},{9,0},... | collective-permute-start | bytes 98312 | tf_op jit(solution)/shard_map/ppermute | solution.py:91
  13.3 0.1 fusion.3
  13.4 0.9 %broadcast_select_fusion = (f32[8,8192]{1,0:T(8,128)}, f32[8,8192]{1,0:T(8,128)}) fusion(f32[8,8192]{1,0:T(8,128)S(1)} %get-tuple-element.44.moment, f32[8192]{0:T(1024)S(1)} %get-tuple-element.53, pred[8]{0:T(512)(128)(4,1)S(1)} %fusion.3, f32[8,8192]{1,0:T(8,128)S(1)} %get-tuple-element.42.outer, f32[8192]{0:T(1024)S(1)} %bitcast.12), kind=kLoop, calls=%fused_computation.6 | loop fusion | flops 131072 | bytes 1114120 | tf_op jit(solution)/shard_map/jit(_where)/select_n | solution.py:232
  14.4 0.0 collective-permute-done.4.got
  14.4 0.9 %collective-permute-start.5 = (bf16[2,64,128]{2,1,0:T(8,128)(2,1)S(1)}, bf16[2,64,128]{2,1,0:T(8,128)(2,1)S(1)}, u32[]{:S(2)}, u32[]{:S(2)}) collective-permute-start(bf16[2,64,128]{2,1,0:T(8,128)(2,1)S(1)} %collective-permute-done.4.got), channel_id=1, source_target_pairs={{0,8},{1,9},{2,10},{3,11},{4,12},{5,13},{6,14},{7,15},{8,0},{9,1},... | collective-permute-start | bytes 98312 | tf_op jit(solution)/shard_map/ppermute | solution.py:91
  15.3 0.8 %add_select_fusion = f32[1,8,8192]{2,1,0:T(8,128)} fusion(f32[1,8,8192]{2,1,0:T(8,128)S(1)} %get-tuple-element.40, f32[8192]{0:T(1024)S(1)} %multiply_bitcast_fusion, pred[8]{0:T(512)(128)(4,1)S(1)} %fusion.3), kind=kLoop, calls=%fused_computation.4 | loop fusion | flops 196608 | bytes 557064 | tf_op jit(solution)/shard_map/jit(_where)/select_n | solution.py:238
  16.1 0.0 collective-permute-done.6.across_1
  16.1 0.1 collective-permute-done.5.other
  16.1 0.7 %order.1 = bf16[512,128]{1,0:T(8,128)(2,1)} custom-call(bf16[2,64,128]{2,1,0:T(8,128)(2,1)S(1)} %pad_maximum_fusion.own, bf16[2,64,128]{2,1,0:T(8,128)(2,1)S(1)} %collective-permute-done.6.across_1, bf16[2,64,128]{2,1,0:T(8,128)(2,1)S(1)} %collective-permute-done.4.got, bf16[2,64,128]{2,1,0:T(8,128)(2,1)S(1)} %collective-permute-done.5.other), custom_call_target="tpu_custom_call" | custom-call | tf_op jit(solution)/shard_map/order/pallas_call | solution.py:152
  (5 shorter events, 0.0 us)
Async XLA Ops:
  0.6 1.9 %collective-permute-start = (f32[8,8192]{1,0:T(8,128)}, f32[8,8192]{1,0:T(8,128)S(1)}, u32[]{:S(2)}, u32[]{:S(2)}) collective-permute-start(f32[8,8192]{1,0:T(8,128)} %bitcast.10), channel_id=1, source_target_pairs={{0,8},{1,9},{2,10},{3,11},{4,12},{5,13},{6,14},{7,15},{8,0},{9,1},... | collective-permute-start | bytes 786440 | tf_op jit(solution)/shard_map/ppermute | solution.py:91
  2.5 5.7 %copy-start = (f32[1,8,8192]{2,1,0:T(8,128)S(1)}, f32[1,8,8192]{2,1,0:T(8,128)}, u32[]{:S(2)}) copy-start(f32[1,8,8192]{2,1,0:T(8,128)} %param.12) | copy-start | bytes 786436
  2.5 5.7 %copy-start.1 = (f32[1,8,8192]{2,1,0:T(8,128)S(1)}, f32[1,8,8192]{2,1,0:T(8,128)}, u32[]{:S(2)}) copy-start(f32[1,8,8192]{2,1,0:T(8,128)} %param.13) | copy-start | bytes 786436
  2.6 5.7 %copy-start.2 = (bf16[1,8,8192]{2,1,0:T(8,128)(2,1)S(1)}, bf16[1,8,8192]{2,1,0:T(8,128)(2,1)}, u32[]{:S(2)}) copy-start(bf16[1,8,8192]{2,1,0:T(8,128)(2,1)} %param.11) | copy-start | bytes 393220
  2.6 4.3 %collective-permute-start.1 = (f32[64,128]{1,0:T(8,128)S(1)}, f32[64,128]{1,0:T(8,128)S(1)}, u32[]{:S(2)}, u32[]{:S(2)}) collective-permute-start(f32[64,128]{1,0:T(8,128)S(1)} %get-tuple-element.56), channel_id=1, source_target_pairs={{0,24},{1,25},{2,26},{3,27},{4,28},{5,29},{6,30},{7,31},{8,18},{9,... | collective-permute-start | bytes 98312 | tf_op jit(solution)/shard_map/ppermute | solution.py:111
  5.3 4.0 %collective-permute-start.3 = (f32[64,128]{1,0:T(8,128)S(1)}, f32[64,128]{1,0:T(8,128)S(1)}, u32[]{:S(2)}, u32[]{:S(2)}) collective-permute-start(f32[64,128]{1,0:T(8,128)S(1)} %get-tuple-element.55), channel_id=1, source_target_pairs={{0,10},{1,11},{2,8},{3,9},{4,14},{5,15},{6,12},{7,13},{8,2},{9,3},... | collective-permute-start | bytes 98312 | tf_op jit(solution)/shard_map/ppermute | solution.py:91
  6.9 2.4 %collective-permute-start.2 = (f32[64,128]{1,0:T(8,128)S(1)}, f32[64,128]{1,0:T(8,128)S(1)}, u32[]{:S(2)}, u32[]{:S(2)}) collective-permute-start(f32[64,128]{1,0:T(8,128)S(1)} %collective-permute-done.1), channel_id=1, source_target_pairs={{0,8},{1,9},{2,10},{3,11},{4,12},{5,13},{6,14},{7,15},{8,0},{9,1},... | collective-permute-start | bytes 98312 | tf_op jit(solution)/shard_map/ppermute | solution.py:91
  9.3 5.0 %collective-permute-start.4 = (bf16[2,64,128]{2,1,0:T(8,128)(2,1)S(1)}, bf16[2,64,128]{2,1,0:T(8,128)(2,1)S(1)}, u32[]{:S(2)}, u32[]{:S(2)}) collective-permute-start(bf16[2,64,128]{2,1,0:T(8,128)(2,1)S(1)} %pad_maximum_fusion.own), channel_id=1, source_target_pairs={{0,12},{1,13},{2,14},{3,15},{4,9},{5,8},{6,11},{7,10},{8,5},{9,4},... | collective-permute-start | bytes 98312 | tf_op jit(solution)/shard_map/ppermute | solution.py:111
  12.3 3.7 %collective-permute-start.6 = (bf16[2,64,128]{2,1,0:T(8,128)(2,1)S(1)}, bf16[2,64,128]{2,1,0:T(8,128)(2,1)S(1)}, u32[]{:S(2)}, u32[]{:S(2)}) collective-permute-start(bf16[2,64,128]{2,1,0:T(8,128)(2,1)S(1)} %pad_maximum_fusion.own), channel_id=1, source_target_pairs={{0,9},{1,8},{2,11},{3,10},{4,13},{5,12},{6,15},{7,14},{8,1},{9,0},... | collective-permute-start | bytes 98312 | tf_op jit(solution)/shard_map/ppermute | solution.py:91
  14.4 1.8 %collective-permute-start.5 = (bf16[2,64,128]{2,1,0:T(8,128)(2,1)S(1)}, bf16[2,64,128]{2,1,0:T(8,128)(2,1)S(1)}, u32[]{:S(2)}, u32[]{:S(2)}) collective-permute-start(bf16[2,64,128]{2,1,0:T(8,128)(2,1)S(1)} %collective-permute-done.4.got), channel_id=1, source_target_pairs={{0,8},{1,9},{2,10},{3,11},{4,12},{5,13},{6,14},{7,15},{8,0},{9,1},... | collective-permute-start | bytes 98312 | tf_op jit(solution)/shard_map/ppermute | solution.py:91
